TPU v7x, 256 devices: a whole 4x4x8 slice. The times are simulated.
256 devices in a mesh: row: 16 (over z, core), col: 4 (over x), rep: 4 (over y).
Axes of the slice: x: 4, y: 4, z: 8, core: 2. Of those that a mesh axis runs over, the one named last changes fastest.
Arguments:
- front: float32 [4096, 256, 256], P(('row', 'col', 'rep')), may hold values from -6 to 6
- pivots: bfloat16 [4, 2, 256, 256], P('rep'), may hold values from -0.375 to 0.375
- upper_link: bfloat16 [4, 256, 256], P('rep'), may hold values from -0.375 to 0.375
- lower_link: bfloat16 [4, 256, 256], P('rep'), may hold values from -0.375 to 0.375
- lower_panels: bfloat16 [4, 2, 32, 256, 256], P('rep', None, 'row', 'col'), may hold values from -6 to 6
- upper_panels: bfloat16 [4, 2, 96, 256, 256], P('rep', None, 'col', 'row'), may hold values from -0.375 to 0.375
- lower_slots: int32 [4, 2, 32], P(None, None, 'row'), may hold values from -1 to 1, as said below
- upper_slots: int32 [4, 2, 96], P(None, None, 'col'), may hold values from -1 to 31, as said below
- owner_map: int32 [64, 64], P(('row', 'col')), may hold values from 0 to 63, each once within a row
Outputs:
- schur: float32 [4096, 256, 256], P(('row', 'col', 'rep'))
Inputs may be any that keep to these rules, and one draw needn't show every extreme that they name: `lower_slots`: for each replica, panel and process row r, the 2 entries from r * 2 on name distinct local block rows, filled entries first and -1 for the empty rest; half of them or more are filled, and in every replica and panel some process row has all filled. `upper_slots`: for each replica, panel and process column c, the 24 entries from c * 24 on name distinct local block columns, filled entries first and -1 for the empty rest; half of them or more are filled, and in every replica and panel some process column has all filled. `owner_map`: row t is a permutation of the local block indices e = a * 32 + b of the tile of process row t // 4 and process column t % 4; entries q * 16 to (q + 1) * 16 - 1 are the blocks whose result replica q holds.
All inputs are finite; a program needn't handle non-finite values.
Results may differ from a plain program's by a relative error of at most 0.0095.
Values may be sent and summed in bfloat16 or wider, within the bound.
A program may use at most 192 MiB of HBM per device.

v0:
```python
import jax
import jax.numpy as jnp
from jax import lax
from jax.sharding import PartitionSpec as P


def matching(later, earlier):
    agreeing = (later[:, None] == earlier[None, :]) & (later[:, None] >= 0)
    return agreeing.astype(jnp.bfloat16)


def select_blocks(chooser, blocks):
    return jnp.einsum("ps,sxy->pxy", chooser, blocks, preferred_element_type=jnp.float32).astype(
        jnp.bfloat16
    )


def body(
    front,
    pivots,
    upper_link,
    lower_link,
    lower_panels,
    upper_panels,
    lower_slots,
    upper_slots,
    owner_map,
):
    replica = lax.axis_index("rep")
    breadth = pivots.shape[-1]
    row_slots = lower_slots.shape[2]
    tile_count = owner_map.shape[1]
    col_blocks = tile_count // row_slots
    own_lower = lax.dynamic_index_in_dim(lower_slots, replica, 0, keepdims=False)
    own_upper = lax.dynamic_index_in_dim(upper_slots, replica, 0, keepdims=False)
    first_pivot = pivots[0, 0]
    second_pivot = pivots[0, 1]
    lower_first = jnp.einsum(
        "sxy,yz->sxz", lower_panels[0, 0], first_pivot, preferred_element_type=jnp.float32
    ).astype(jnp.bfloat16)
    lower_carried = select_blocks(matching(own_lower[1], own_lower[0]), lower_first)
    carried_term = jnp.einsum(
        "sxy,yz->sxz", lower_carried, upper_link[0], preferred_element_type=jnp.float32
    )
    lower_diff = (lower_panels[0, 1].astype(jnp.float32) - carried_term).astype(jnp.bfloat16)
    lower_second = jnp.einsum(
        "sxy,yz->sxz", lower_diff, second_pivot, preferred_element_type=jnp.float32
    ).astype(jnp.bfloat16)
    lower_whole = lax.all_gather(jnp.stack([lower_first, lower_second]), "col", axis=2, tiled=True)
    link_row = jnp.dot(lower_link[0], first_pivot, preferred_element_type=jnp.float32).astype(
        jnp.bfloat16
    )
    same_cols = matching(own_upper[1], own_upper[0])
    upper_whole = lax.all_gather(upper_panels[0], "row", axis=2, tiled=True)
    upper_first = upper_whole[0]
    upper_carried = select_blocks(same_cols, upper_first)
    shifted = jnp.einsum("xy,tyz->txz", link_row, upper_carried, preferred_element_type=jnp.float32)
    upper_second = (upper_whole[1].astype(jnp.float32) - shifted).astype(jnp.bfloat16)
    usable = (own_lower[:, :, None] >= 0) & (own_upper[:, None, :] >= 0)
    places = jnp.where(
        usable, own_lower[:, :, None] * col_blocks + own_upper[:, None, :], tile_count
    )
    tile_sum = jnp.zeros((tile_count, breadth, breadth), jnp.float32)
    upper_pair = (upper_first, upper_second)
    for panel_index in range(2):
        products = jnp.einsum(
            "sxy,tyz->stxz",
            lower_whole[panel_index],
            upper_pair[panel_index],
            preferred_element_type=jnp.float32,
        )
        tile_sum = tile_sum.at[places[panel_index].reshape(-1)].add(
            products.reshape(-1, breadth, breadth), mode="drop"
        )
    ordered = jnp.take(tile_sum, owner_map[0], axis=0)
    summed = lax.psum_scatter(
        ordered.astype(jnp.bfloat16), "rep", scatter_dimension=0, tiled=True
    ).astype(jnp.float32)
    return front - summed


def solution(mesh):
    return jax.shard_map(
        body,
        mesh=mesh,
        in_specs=(
            P(("row", "col", "rep"), None, None),
            P("rep", None, None, None),
            P("rep", None, None),
            P("rep", None, None),
            P("rep", None, "row", "col", None),
            P("rep", None, "col", "row", None),
            P(None, None, "row"),
            P(None, None, "col"),
            P(("row", "col"), None),
        ),
        out_specs=P(("row", "col", "rep"), None, None),
        check_vma=False,
    )
```

profile of v0, /device:TPU:1, one launch (start us, length us, event | category | flops | bytes accessed | tf_op | source)
XLA Modules:
  0.0 270.4 jit_solution(7915777432722782604)
XLA Ops:
  6.5 0.0 copy-start
  6.5 0.0 all-gather.3.cloned.1.call-start
  6.5 0.7 all-gather.3.cloned.1.call-update
  7.3 0.0 reduce-scatter.2.cloned.1.call-start
  7.3 0.9 multiply_reduce_fusion
  8.2 0.9 compare_reduce_fusion
  9.1 0.7 broadcast_compare_fusion
  9.8 0.1 and_select_fusion
  9.9 0.1 reshape_squeeze.6
  10.0 0.1 reshape_squeeze.7
  10.1 0.9 dynamic-slice_reduce_fusion
  11.0 0.7 fusion.38
  11.6 1.1 convolution_convert_fusion.2
  12.8 0.3 fusion.26
  13.0 1.3 fusion.11
  14.4 0.0 copy-done
  14.4 1.1 fusion.9
  15.5 12.8 %all_gather.6 = bf16[2,2,256,256]{3,2,1,0:T(8,128)(2,1)} all-gather(bf16[2,2,64,256]{3,2,1,0:T(8,128)(2,1)S(1)} %pad_maximum_fusion), channel_id=1, replica_groups=mesh['row'=16,'col'=4,'rep'=4] {'col'}, dimensions={2}, use_global_device_ids=true | all-gather | bytes 655360 | tf_op jit(solution)/shard_map/all_gather | solution.py:49
  28.3 0.7 compare_and_fusion
  29.0 30.6 %all-gather.3.cloned.1.call-done = bf16[1,2,24,256,256]{4,3,2,1,0:T(8,128)(2,1)} async-done(((bf16[1,2,24,16,256]{4,3,2,1,0:T(8,128)(2,1)}), bf16[1,2,24,256,256]{4,3,2,1,0:T(8,128)(2,1)}) %all-gather.3.cloned.1.call-update) | async-done | bytes 6291472 | tf_op jit(solution)/shard_map/all_gather | solution.py:54
  59.5 2.2 slice_bitcast_fusion.2
  61.7 2.4 fusion.6
  64.1 7.6 %convolution_bitcast_fusion = f32[2,24,256,256]{2,3,0,1:T(8,128)} fusion(bf16[1,2,24,256,256]{4,3,2,1,0:T(8,128)(2,1)} %all-gather.3.cloned.1.call-done, bf16[256,256,1]{1,0,2:T(8,128)(2,1)S(1)} %fusion.9, bf16[24,256,256]{2,0,1:T(8,128)(2,1)S(1)} %fusion.6, bf16[2,2,256,256]{3,2,1,0:T(8,128)(2,1)} %all_gather.6), kind=kOutput, calls=%fused_computation.7 | convolution fusion | flops 2420637696 | bytes 19267584 | tf_op jit(solution)/shard_map/sxy,tyz->stxz/dot_general | solution.py:66
  71.7 0.0 copy-start.2
  71.7 12.6 %copy.12 = f32[2,24,256,256]{3,2,1,0:T(8,128)} copy(f32[2,24,256,256]{2,3,0,1:T(8,128)} %convolution_bitcast_fusion) | data formatting | bytes 25165824 | tf_op jit(solution)/shard_map/sxy,tyz->stxz/transpose | solution.py:66
  84.3 0.0 copy-done.2
  84.3 8.1 %fusion.4 = f32[2,256,24,256]{3,1,2,0:T(8,128)} fusion(bf16[1,2,24,256,256]{4,3,2,1,0:T(8,128)(2,1)} %all-gather.3.cloned.1.call-done, bf16[2,2,256,256]{3,2,1,0:T(8,128)(2,1)S(1)} %copy-done.2), kind=kOutput, calls=%fused_computation.12 | convolution fusion | flops 1610612736 | bytes 15990784 | tf_op jit(solution)/shard_map/sxy,tyz->stxz/dot_general | solution.py:66
  92.5 7.9 %broadcast_in_dim.26 = f32[64,256,256]{2,1,0:T(8,128)} broadcast(f32[]{:T(128)} %constant.16.clone.1), dimensions={} | broadcast | bytes 16777220 | tf_op jit(solution)/shard_map/broadcast_in_dim | solution.py:63
  100.3 24.2 %scatter_fusion = f32[64,256,256]{2,1,0:T(8,128)} fusion(f32[64,256,256]{2,1,0:T(8,128)} %broadcast_in_dim.26, s32[48]{0:T(128)S(1)} %fusion.36, f32[48,256,256]{2,1,0:T(8,128)} %bitcast.97), kind=kCustom, calls=%fused_computation.1 | custom fusion | flops 3145728 | bytes 37748928 | tf_op jit(solution)/shard_map/scatter-add | solution.py:72
  124.6 27.4 %scatter_fusion.1 = f32[64,256,256]{2,1,0:T(8,128)} fusion(f32[64,256,256]{2,1,0:T(8,128)} %scatter_fusion, s32[48]{0:T(128)S(1)} %fusion.37, f32[48,256,256]{2,1,0:T(8,128)} %bitcast.98), kind=kCustom, calls=%fused_computation.2 | custom fusion | flops 3145728 | bytes 37748928 | tf_op jit(solution)/shard_map/scatter-add | solution.py:72
  152.0 11.9 %gather_fusion = bf16[64,256,256]{2,1,0:T(8,128)(2,1)} fusion(f32[64,256,256]{2,1,0:T(8,128)} %scatter_fusion.1, s32[1024]{0:T(1024)S(1)} %pad_clamp_fusion), kind=kCustom, calls=%fused_computation | custom fusion | bytes 16777472 | tf_op jit(solution)/shard_map/jit(_take)/gather | solution.py:75
  164.0 10.1 %select_convert_fusion = bf16[64,256,256]{2,1,0:T(8,128)(2,1)} fusion(bf16[64,256,256]{2,1,0:T(8,128)(2,1)} %gather_fusion, pred[64]{0:T(512)(128)(4,1)S(1)} %compare_and_fusion), kind=kLoop, calls=%fused_computation.3 | loop fusion | flops 4194304 | bytes 16777280 | tf_op jit(solution)/shard_map/convert_element_type | solution.py:77
  174.0 0.0 reduce-scatter.2.cloned.1.call-update
  174.0 0.0 copy-start.1
  174.1 84.2 %reduce-scatter.2.cloned.1.call-done = bf16[16,256,256]{2,1,0:T(8,128)(2,1)} async-done(((bf16[64,256,256]{2,1,0:T(8,128)(2,1)}), bf16[16,256,256]{2,1,0:T(8,128)(2,1)}) %reduce-scatter.2.cloned.1.call-update) | async-done | bytes 2097168 | tf_op jit(solution)/shard_map/reduce_scatter | solution.py:76
  258.2 5.4 %convert_subtract_fusion.1 = f32[16,256,256]{2,1,0:T(8,128)} fusion(f32[16,256,256]{2,1,0:T(8,128)} %param.9, bf16[16,256,256]{2,1,0:T(8,128)(2,1)} %reduce-scatter.2.cloned.1.call-done), kind=kLoop, calls=%fused_computation.8 | loop fusion | flops 2097152 | bytes 10485760 | tf_op jit(solution)/shard_map/sub | solution.py:79
  263.6 0.0 copy-done.1
  (8 shorter events, 0.1 us)
Async XLA Ops:
  6.5 7.8 %copy-start = (bf16[1,256,256]{2,1,0:T(8,128)(2,1)S(1)}, bf16[1,256,256]{2,1,0:T(8,128)(2,1)}, u32[]{:S(2)}) copy-start(bf16[1,256,256]{2,1,0:T(8,128)(2,1)} %param.12) | copy-start | bytes 393220
  6.5 53.0 %all-gather.3.cloned.1.call-start = ((), (), s32[]{:S(2)}) async-start(), calls=%async_computation.2 | async-start | bytes 6684672 | tf_op jit(solution)/shard_map/all_gather | solution.py:54
  7.3 251.0 %reduce-scatter.2.cloned.1.call-start = ((), (), s32[]{:S(2)}) async-start(), calls=%async_computation.1 | async-start | bytes 10485760 | tf_op jit(solution)/shard_map/reduce_scatter | solution.py:76
  71.7 12.7 %copy-start.2 = (bf16[2,2,256,256]{3,2,1,0:T(8,128)(2,1)S(1)}, bf16[2,2,256,256]{3,2,1,0:T(8,128)(2,1)}, u32[]{:S(2)}) copy-start(bf16[2,2,256,256]{3,2,1,0:T(8,128)(2,1)} %all_gather.6) | copy-start | bytes 1572868
  174.0 89.5 %copy-start.1 = (bf16[1,256,256]{2,1,0:T(8,128)(2,1)S(1)}, bf16[1,256,256]{2,1,0:T(8,128)(2,1)}, u32[]{:S(2)}) copy-start(bf16[1,256,256]{2,1,0:T(8,128)(2,1)} %param.12) | copy-start | bytes 393220
Sparse Core Ops, SparseCore 0:
  9.2 50.2 all-gather.2
  174.2 84.0 reduce-scatter.1
where the time goes:
time: 271 us; the launch traced here: 270 us
  waiting for transfers between devices  115 us (42%)
  other arithmetic  71 us (26%)
  local copies, waits for them, and re-layouts  35.8 us (13%)
  matrix products  21.9 us (8%)
  between operations  13.5 us (5%)
  blocking collectives  12.8 us (5%)
    reduce_scatter x1, waiting for transfers between devices, body(): lax.psum_scatter(ordered.astype(jnp.bfloat16), 'rep', scatter_dimension=0...  84.2 us
    scatter-add x2, other arithmetic, body(): tile_sum.at[places[panel_index].reshape(-1)]  51.7 us
    all_gather x1, waiting for transfers between devices, body(): upper_whole = lax.all_gather(upper_panels[0], 'row', axis=2, tiled=True)  30.6 us
    dot_general x2, matrix products, body(): jnp.einsum('sxy,tyz->stxz', lower_whole[panel_index], upper_pair[panel_in...  15.7 us
    all_gather x1, blocking collectives, body(): lax.all_gather(jnp.stack([lower_first, lower_second]), 'col', axis=2, til...  12.8 us
    transpose x1, local copies, waits for them, and re-layouts, body(): jnp.einsum('sxy,tyz->stxz', lower_whole[panel_index], upper_pair[panel_in...  12.6 us
    gather x1, local copies, waits for them, and re-layouts, body(): ordered = jnp.take(tile_sum, owner_map[0], axis=0)  11.9 us
    convert_element_type x1, other arithmetic, body(): ordered.astype(jnp.bfloat16)  10.1 us
  transfers between devices with their start and end apart: 2, of which 2 were waited for; matrix products, arithmetic and copies ran while one was open for 3% of the time, Pallas kernels for 0%

commit v1 on v0

v1 whole, which is shorter than its diff:
```python
import functools

import jax
import jax.numpy as jnp
from jax import lax
from jax.experimental import pallas as pl
from jax.experimental.pallas import tpu as pltpu
from jax.sharding import PartitionSpec as P

MESH = pl.DeviceIdType.MESH
NT = (((1,), (1,)), ((), ()))
B = 256
CH = 2
W = 32
SLOTS = 24
GROUPS = 6
SUBS = (0, 1, 3, 2)
LAST = ((0, 1), (2, 3))
ZN = 8


def main_kernel(
    inv_ref,
    lsl_ref,
    own_ref,
    u_ref,
    lp_ref,
    piv_ref,
    ul_ref,
    ll_ref,
    out_ref,
    pk,
    ug,
    ut,
    lb,
    lsel,
    lhs,
    acb,
    ctb,
    snd,
    a2a_s,
    a2a_r,
    ring_s,
    ring_r,
    sib_s,
    sib_r,
    ly_s,
    ly_r,
    lx_s,
    lx_r,
    shp_s,
    shp_r,
    loc_s,
):
    row = lax.axis_index("row")
    x = lax.axis_index("col")
    y = lax.axis_index("rep")
    z = row // 2
    core = row % 2

    def ydev(d):
        return (row, x, (y + d) % 4)

    def xdev(d):
        return (row, (x + d) % 4, y)

    def zdev(d):
        return (((z + d + ZN) % ZN) * 2 + core, x, y)

    sib = (z * 2 + 1 - core, x, y)

    def src_of(d):
        return ((z + d + ZN) % ZN) * 2 + core

    def rep_of(sub):
        return (y - SUBS[sub] + 4) % 4

    bar = pltpu.get_barrier_semaphore()
    partners = [ydev(1), ydev(2), ydev(3), xdev(1), xdev(2), xdev(3), zdev(1), zdev(-1), sib]
    for p in partners:
        pl.semaphore_signal(bar, inc=1, device_id=p, device_id_type=MESH)

    def pack(ch):
        parts = [
            u_ref[:, :, j, :, 128 * ch : 128 * ch + 128].reshape(2 * GROUPS * 16, 128)
            for j in range(4)
        ]
        for yy in range(4):
            piece = jnp.concatenate([p[:, W * yy : W * yy + W] for p in parts], axis=1)
            pk[ch, yy] = piece.reshape(2, GROUPS, 16, 128)

    def remote(src, dst, ss, rs, dev):
        return pltpu.make_async_remote_copy(
            src_ref=src, dst_ref=dst, send_sem=ss, recv_sem=rs, device_id=dev, device_id_type=MESH
        )

    def a2a(ch, sub, receive=False):
        d = SUBS[sub]
        if receive:
            ref = ug.at[ch, row, rep_of(sub)]
            return remote(ref, ref, a2a_s.at[ch, sub - 1], a2a_r.at[ch, sub - 1], ydev(d))
        return remote(
            pk.at[ch, (y + d) % 4],
            ug.at[ch, row, y],
            a2a_s.at[ch, sub - 1],
            a2a_r.at[ch, sub - 1],
            ydev(d),
        )

    def ring(ch, way, step, sub, receive=False):
        sign = 1 if way == 0 else -1
        origin = src_of(-sign * (step + 1 if receive else step))
        ref = ug.at[ch, origin, rep_of(sub)]
        return remote(
            ref, ref, ring_s.at[ch, way, step, sub], ring_r.at[ch, way, step, sub], zdev(sign)
        )

    def sibling(ch, d, receive=False):
        s = (z + d + ZN) % ZN
        ref = ug.at[ch, s * 2 + (1 - core if receive else core)]
        return remote(ref, ref, sib_s.at[ch, d % ZN], sib_r.at[ch, d % ZN], sib)

    def ring_subs(way, step):
        return range(4) if step < 3 else LAST[way]

    def ring_first(ch, subs):
        for sub in subs:
            if sub:
                a2a(ch, sub, True).wait_recv()
            for way in range(2):
                ring(ch, way, 0, sub).start()

    def ring_step(ch, step):
        for sub in range(4):
            for way in range(2):
                if sub in ring_subs(way, step - 1):
                    ring(ch, way, step - 1, sub, True).wait_recv()
                    if step < 4 and sub in ring_subs(way, step):
                        ring(ch, way, step, sub).start()
        if step < 4:
            sibling(ch, -step).start()
            sibling(ch, step).start()
        else:
            sibling(ch, 4).start()

    def ly(sub, receive=False):
        d = SUBS[sub]
        ref = lb.at[rep_of(sub) if receive else y, x, pl.ds(0, 5)]
        return remote(ref, ref, ly_s.at[sub - 1], ly_r.at[sub - 1], ydev(d))

    def lx(sub, d, receive=False):
        ref = lb.at[rep_of(sub), (x - d + 4) % 4 if receive else x, pl.ds(0, 5)]
        return remote(ref, ref, lx_s.at[sub, d - 1], lx_r.at[sub, d - 1], xdev(d))

    def ship(ch, d, receive=False):
        if receive:
            ref = out_ref.at[ch, (y - d + 4) % 4]
            return remote(ref, ref, shp_s.at[ch, d - 1], shp_r.at[ch, d - 1], ydev(d))
        return remote(
            snd.at[ch, (y + d) % 4],
            out_ref.at[ch, y],
            shp_s.at[ch, d - 1],
            shp_r.at[ch, d - 1],
            ydev(d),
        )

    def lower_prep():
        first = jnp.dot(
            lp_ref[0].reshape(128, B), piv_ref[0], preferred_element_type=jnp.float32
        ).astype(jnp.bfloat16)
        lb[y, x, 0:2] = first.reshape(2, 64, B)
        wide = first.astype(jnp.float32)
        pieces = []
        for g in range(2):
            sg = lsl_ref[y * 2 + 1, g]
            hit0 = jnp.where((sg >= 0) & (sg == lsl_ref[y * 2, 0]), 1.0, 0.0)
            hit1 = jnp.where((sg >= 0) & (sg == lsl_ref[y * 2, 1]), 1.0, 0.0)
            pieces.append(wide[:64] * hit0 + wide[64:] * hit1)
        carried = jnp.concatenate(pieces, axis=0).astype(jnp.bfloat16)
        term = jnp.dot(carried, ul_ref[...], preferred_element_type=jnp.float32)
        diff = (lp_ref[1].reshape(128, B).astype(jnp.float32) - term).astype(jnp.bfloat16)
        second = jnp.dot(diff, piv_ref[1], preferred_element_type=jnp.float32).astype(jnp.bfloat16)
        lb[y, x, 2:4] = second.reshape(2, 64, B)
        link = jnp.dot(
            ll_ref[pl.ds(pl.multiple_of(x * 64, 64), 64), :],
            piv_ref[0],
            preferred_element_type=jnp.float32,
        ).astype(jnp.bfloat16)
        lb[y, x, 4] = link
        for q in range(4):
            for xx in range(4):
                lb[q, xx, 5] = jnp.zeros((64, B), jnp.bfloat16)

    def lower_select():
        for q in range(4):
            for k in range(2):
                s0 = lsl_ref[q * 2 + k, 0]
                s1 = lsl_ref[q * 2 + k, 1]
                for a in range(2):
                    at = jnp.where(s0 == a, 2 * k, jnp.where(s1 == a, 2 * k + 1, 5))
                    for xx in range(4):
                        lsel[
                            a * B + xx * 64 : a * B + xx * 64 + 64,
                            (2 * q + k) * B : (2 * q + k + 1) * B,
                        ] = lb[q, xx, at]

    def turn(ch):
        def step(i, carry):
            q, k = i // 2, i % 2
            for g in range(GROUPS):
                block = ug[ch, :, q, k, g].reshape(B, 128)
                ut[q, k, 4 * g : 4 * g + 4] = block.T.reshape(4, W, B)
            return carry

        lax.fori_loop(0, 8, step, 0)

    def arrange():
        def step(b, carry):
            for q in range(4):
                at0 = inv_ref[q * 3, b]
                at1 = inv_ref[q * 3 + 1, b]
                atc = inv_ref[q * 3 + 2, b]
                rows = pl.ds(pl.multiple_of(b * W, W), W)
                lhs[rows, 2 * q * B : 2 * q * B + B] = ut[q, 0, at0]
                lhs[rows, (2 * q + 1) * B : (2 * q + 2) * B] = ut[q, 1, at1]
                acb[q, rows, :] = ut[q, 0, atc]
            return carry

        lax.fori_loop(0, 32, step, 0)

    def second_upper():
        for q in range(4):
            link = lb[q, :, 4].reshape(B, B)

            def step(i, carry):
                rows = pl.ds(pl.multiple_of(i * 256, 256), 256)
                shift = lax.dot_general(
                    acb[q, rows, :], link, NT, preferred_element_type=jnp.float32
                )
                cols = slice((2 * q + 1) * B, (2 * q + 2) * B)
                lhs[rows, cols] = (lhs[rows, cols].astype(jnp.float32) - shift).astype(jnp.bfloat16)
                return carry

            lax.fori_loop(0, 4, step, 0)

    def multiply():
        def step(i, carry):
            rows = pl.ds(pl.multiple_of(i * 256, 256), 256)
            prod = lax.dot_general(
                lhs[rows, :], lsel[...], NT, preferred_element_type=jnp.float32
            ).astype(jnp.bfloat16)
            for a in range(2):
                ctb[a, pl.ds(i * 8, 8)] = prod[:, a * B : a * B + B].reshape(8, W, B)
            return carry

        lax.fori_loop(0, 4, step, 0)

    def choose(ch):
        def step(m, carry):
            e = own_ref[0, m]
            snd[ch, m // 16, m % 16] = ctb[e // 32, e % 32]
            return carry

        lax.fori_loop(0, 64, step, 0)

    def local_out(ch):
        return pltpu.make_async_copy(snd.at[ch, y], out_ref.at[ch, y], loc_s.at[ch])

    def start_ship(ch):
        for d in (1, 3, 2):
            ship(ch, d).start()
        local_out(ch).start()

    def wait_sibling(ch):
        for d in range(ZN):
            sibling(ch, d if d < 5 else d - ZN, True).wait_recv()

    for q in range(4):
        for k in range(2):
            ut[q, k, SLOTS] = jnp.zeros((W, B), jnp.bfloat16)
    pack(0)
    ug[0, row, y] = pk[0, y]
    pl.semaphore_wait(bar, len(partners))
    for sub in (1, 2, 3):
        a2a(0, sub).start()
    ring_first(0, (0,))
    lower_prep()
    for sub in (1, 2, 3):
        ly(sub).start()
    for d in (1, 3, 2):
        lx(0, d).start()
    pack(1)
    ug[1, row, y] = pk[1, y]
    for sub in (1, 2, 3):
        a2a(1, sub).start()
    ring_first(0, (1, 2, 3))
    sibling(0, 0).start()
    for sub in (1, 2, 3):
        ly(sub, True).wait_recv()
        for d in (1, 3, 2):
            lx(sub, d).start()
    ring_step(0, 1)
    ring_step(0, 2)
    ring_step(0, 3)
    ring_first(1, (0, 1, 2, 3))
    sibling(1, 0).start()
    for sub in range(4):
        for d in (1, 3, 2):
            lx(sub, d, True).wait_recv()
    lower_select()
    ring_step(0, 4)
    ring_step(1, 1)
    wait_sibling(0)
    turn(0)
    arrange()
    second_upper()
    ring_step(1, 2)
    multiply()
    choose(0)
    start_ship(0)
    ring_step(1, 3)
    ring_step(1, 4)
    wait_sibling(1)
    turn(1)
    arrange()
    second_upper()
    multiply()
    choose(1)
    start_ship(1)

    for ch in range(CH):
        for sub in (1, 2, 3):
            a2a(ch, sub).wait_send()
        for way in range(2):
            for st in range(4):
                for sub in ring_subs(way, st):
                    ring(ch, way, st, sub).wait_send()
        for d in range(ZN):
            sibling(ch, d if d < 5 else d - ZN).wait_send()
    for sub in range(4):
        if sub:
            ly(sub).wait_send()
        for d in (1, 2, 3):
            lx(sub, d).wait_send()
    for ch in range(CH):
        local_out(ch).wait()
        for d in (1, 2, 3):
            ship(ch, d).wait_send()
            ship(ch, d, True).wait_recv()


def finish_kernel(front_ref, got_ref, out_ref):
    for i in range(front_ref.shape[0]):
        block = got_ref[:, :, i].reshape(B, B)
        out_ref[i] = front_ref[i] - block.T.astype(jnp.float32)


def body(
    front,
    pivots,
    upper_link,
    lower_link,
    lower_panels,
    upper_panels,
    lower_slots,
    upper_slots,
    owner_map,
):
    names = jnp.arange(32, dtype=jnp.int32)
    same = upper_slots[:, :, None, :] == names[None, None, :, None]
    at = jnp.arange(SLOTS, dtype=jnp.int32)
    inv = jnp.min(jnp.where(same, at[None, None, None, :], SLOTS), axis=-1)
    carried = jnp.where(inv[:, 1] < SLOTS, inv[:, 0], SLOTS)
    inv = jnp.concatenate([inv, carried[:, None]], axis=1).reshape(12, 32)
    vmem = pl.BlockSpec(memory_space=pltpu.VMEM)
    smem = pl.BlockSpec(memory_space=pltpu.SMEM)
    dma = pltpu.SemaphoreType.DMA
    bf = jnp.bfloat16
    got = pl.pallas_call(
        main_kernel,
        out_shape=jax.ShapeDtypeStruct((CH, 4, 16, W, B), bf),
        in_specs=[smem] * 3 + [vmem] * 5,
        out_specs=pl.BlockSpec(memory_space=pl.ANY),
        scratch_shapes=[
            pltpu.VMEM((CH, 4, 2, GROUPS, 16, 128), bf),
            pltpu.VMEM((CH, 16, 4, 2, GROUPS, 16, 128), bf),
            pltpu.VMEM((4, 2, SLOTS + 1, W, B), bf),
            pltpu.VMEM((4, 4, 6, 64, B), bf),
            pltpu.VMEM((2 * B, 8 * B), bf),
            pltpu.VMEM((32 * W, 8 * B), bf),
            pltpu.VMEM((4, 32 * W, B), bf),
            pltpu.VMEM((2, 32, W, B), bf),
            pltpu.VMEM((CH, 4, 16, W, B), bf),
            dma((CH, 3)),
            dma((CH, 3)),
            dma((CH, 2, 4, 4)),
            dma((CH, 2, 4, 4)),
            dma((CH, ZN)),
            dma((CH, ZN)),
            dma((3,)),
            dma((3,)),
            dma((4, 3)),
            dma((4, 3)),
            dma((CH, 3)),
            dma((CH, 3)),
            dma((CH,)),
        ],
        compiler_params=pltpu.CompilerParams(
            collective_id=0, has_side_effects=True, vmem_limit_bytes=48 << 20
        ),
    )(
        inv,
        lower_slots.reshape(8, 2),
        owner_map,
        upper_panels[0].reshape(2, GROUPS, 4, 16, B),
        lower_panels[0],
        pivots[0],
        upper_link[0],
        lower_link[0],
    )
    return pl.pallas_call(
        finish_kernel,
        grid=(8,),
        out_shape=jax.ShapeDtypeStruct(front.shape, front.dtype),
        in_specs=[
            pl.BlockSpec((2, B, B), lambda i: (i, 0, 0)),
            pl.BlockSpec((CH, 4, 2, W, B), lambda i: (0, 0, i, 0, 0)),
        ],
        out_specs=pl.BlockSpec((2, B, B), lambda i: (i, 0, 0)),
    )(front, got)


def solution(mesh):
    return jax.shard_map(
        body,
        mesh=mesh,
        in_specs=(
            P(("row", "col", "rep"), None, None),
            P("rep", None, None, None),
            P("rep", None, None),
            P("rep", None, None),
            P("rep", None, "row", "col", None),
            P("rep", None, "col", "row", None),
            P(None, None, "row"),
            P(None, None, "col"),
            P(("row", "col"), None),
        ),
        out_specs=P(("row", "col", "rep"), None, None),
        check_vma=False,
    )
```

time: 271 us -> 99.4 us (0.37)
  waiting for transfers between devices: 115 us -> 0 us
  Pallas kernels: 0 us -> 90.8 us
  other arithmetic: 71 us -> 0.81 us
  local copies, waits for them, and re-layouts: 35.8 us -> 7.42 us
  matrix products: 21.9 us -> 0 us
  between operations: 13.5 us -> 0.05 us
  blocking collectives: 12.8 us -> 0 us
    pallas_call x0 -> x2, Pallas kernels: none -> 90.8 us  [the longest x1 83.5 us: body(): pl.pallas_call(main_kernel, out_shape=jax.ShapeDtypeStruct((CH, 4, 16, W,...]
    reduce_scatter x1 -> x0, waiting for transfers between devices: 84.2 us -> none  [body(): lax.psum_scatter(ordered.astype(jnp.bfloat16), 'rep', scatter_dimension=0...]
    scatter-add x2 -> x0, other arithmetic: 51.7 us -> none  [body(): tile_sum.at[places[panel_index].reshape(-1)]]
    all_gather x1 -> x0, waiting for transfers between devices: 30.6 us -> none  [body(): upper_whole = lax.all_gather(upper_panels[0], 'row', axis=2, tiled=True)]
    dot_general x7 -> x0, matrix products: 21.9 us -> none  [the longest x2 15.7 us: body(): jnp.einsum('sxy,tyz->stxz', lower_whole[panel_index], upper_pair[panel_in...]
    all_gather x1 -> x0, blocking collectives: 12.8 us -> none  [body(): lax.all_gather(jnp.stack([lower_first, lower_second]), 'col', axis=2, til...]
    transpose x1 -> x0, local copies, waits for them, and re-layouts: 12.6 us -> none  [body(): jnp.einsum('sxy,tyz->stxz', lower_whole[panel_index], upper_pair[panel_in...]
    gather x1 -> x0, local copies, waits for them, and re-layouts: 11.9 us -> none  [body(): ordered = jnp.take(tile_sum, owner_map[0], axis=0)]
  transfers between devices with their start and end apart: 2 -> 0, of which waited for: 2 -> 0; matrix products, arithmetic and copies ran while one was open for 3% -> 0% of each run, Pallas kernels for 0% -> 0%
where the time goes in v1:
time: 99.4 us; the launch traced here: 99 us
  Pallas kernels  90.8 us (91%)
  local copies, waits for them, and re-layouts  7.42 us (7%)
    pallas_call x1, Pallas kernels, body(): pl.pallas_call(main_kernel, out_shape=jax.ShapeDtypeStruct((CH, 4, 16, W,...  83.5 us
    pallas_call x1, Pallas kernels, body(): pl.pallas_call(finish_kernel, grid=(8,), out_shape=jax.ShapeDtypeStruct(f...  7.24 us
    unnamed x14, local copies, waits for them, and re-layouts  6.63 us

profile of v1, /device:TPU:1, one launch (start us, length us, event | category | flops | bytes accessed | tf_op | source)
XLA Modules:
  0.0 99.0 jit_solution(1271935845297989106)
XLA Ops:
  0.0 0.8 select_reduce_fusion
  0.8 0.8 copy.16
  1.6 0.0 copy-start.1
  1.6 1.0 %copy-done.1 = bf16[1,2,24,16,256]{4,3,2,1,0:T(8,128)(2,1)S(1)} copy-done((bf16[1,2,24,16,256]{4,3,2,1,0:T(8,128)(2,1)S(1)}, bf16[1,2,24,16,256]{4,3,2,1,0:T(8,128)(2,1)}, u32[]{:S(2)}) %copy-start.1) | copy-done | bytes 393240
  2.6 0.0 copy-start.2
  2.6 0.9 copy-done.2
  3.6 0.0 copy-start.3
  3.6 0.9 copy-done.3
  4.5 0.0 copy-start.4
  4.5 0.9 copy-done.4
  5.4 0.0 copy-start.5
  5.4 0.9 copy-done.5
  6.3 0.0 copy-start.6
  6.3 0.7 copy-done.6
  6.9 83.5 %shard_map.91.got_ref = bf16[2,4,16,32,256]{4,3,2,1,0:T(8,128)(2,1)S(1)} custom-call(s32[12,32]{1,0:T(8,128)S(1)} %reshape.7.inv_ref, s32[8,2]{1,0:T(8,128)S(1)} %bitcast.11, s32[1,64]{1,0:T(1,128)S(1)} %copy-done.6, bf16[2,6,4,16,256]{4,3,2,1,0:T(8,128)(2,1)S(1)} %bitcast.6, bf16[2,2,64,256]{3,2,1,0:T(8,128)(2,1)S(1)} %bitcast.8, ...), custom_call_target="tpu_custom_call" | custom-call | tf_op jit(solution)/shard_map/pallas_call | solution.py:379
  90.5 0.0 copy-start
  90.5 1.3 %copy-done = bf16[2,4,16,32,256]{4,3,2,1,0:T(8,128)(2,1)} copy-done((bf16[2,4,16,32,256]{4,3,2,1,0:T(8,128)(2,1)}, bf16[2,4,16,32,256]{4,3,2,1,0:T(8,128)(2,1)S(1)}, u32[]{:S(2)}) %copy-start) | copy-done | bytes 2097176
  91.8 7.2 %shard_map.92 = f32[16,256,256]{2,1,0:T(8,128)} custom-call(f32[16,256,256]{2,1,0:T(8,128)} %front_ref.1, bf16[2,4,16,32,256]{4,3,2,1,0:T(8,128)(2,1)} %copy-done), custom_call_target="tpu_custom_call" | custom-call | tf_op jit(solution)/shard_map/pallas_call | solution.py:421
  (3 shorter events, 0.0 us)
Async XLA Ops:
  1.6 1.0 %copy-start.1 = (bf16[1,2,24,16,256]{4,3,2,1,0:T(8,128)(2,1)S(1)}, bf16[1,2,24,16,256]{4,3,2,1,0:T(8,128)(2,1)}, u32[]{:S(2)}) copy-start(bf16[1,2,24,16,256]{4,3,2,1,0:T(8,128)(2,1)} %param.14) | copy-start | bytes 1179652
  2.6 0.9 copy-start.2
  3.6 0.9 copy-start.3
  4.5 0.9 copy-start.4
  5.4 0.9 copy-start.5
  6.3 0.7 copy-start.6
  90.5 1.3 %copy-start = (bf16[2,4,16,32,256]{4,3,2,1,0:T(8,128)(2,1)}, bf16[2,4,16,32,256]{4,3,2,1,0:T(8,128)(2,1)S(1)}, u32[]{:S(2)}) copy-start(bf16[2,4,16,32,256]{4,3,2,1,0:T(8,128)(2,1)S(1)} %shard_map.91.got_ref) | copy-start | bytes 6291460

commit v2 on v1

v2 whole, which is shorter than its diff:
```python
import jax
import jax.numpy as jnp
from jax import lax
from jax.experimental import pallas as pl
from jax.experimental.pallas import tpu as pltpu
from jax.sharding import PartitionSpec as P

MESH = pl.DeviceIdType.MESH
NT = (((1,), (1,)), ((), ()))
B = 256
CH = 4
W = 16
SLOTS = 24
GS = 8
GROUPS = 3
SUBS = (0, 1, 3, 2)
ZN = 8
TABLE = 16


def main_kernel(
    tab_ref,
    u_hbm,
    lp_hbm,
    piv_hbm,
    ul_hbm,
    ll_hbm,
    out_ref,
    u_ref,
    lp_ref,
    piv_ref,
    ul_ref,
    ll_ref,
    pk,
    ug,
    ut,
    la,
    lb,
    lsel,
    lhs,
    acb,
    ctb,
    snd,
    in_s,
    a2a_s,
    a2a_r,
    ring_s,
    ring_r,
    sib_s,
    sib_r,
    a1_s,
    a1_r,
    a2_s,
    a2_r,
    b1_s,
    b1_r,
    b2_s,
    b2_r,
    shp_s,
    shp_r,
    loc_s,
):
    row = lax.axis_index("row")
    x = lax.axis_index("col")
    y = lax.axis_index("rep")
    z = row // 2
    core = row % 2

    def ydev(d):
        return (row, x, (y + d) % 4)

    def xdev(d):
        return (row, (x + d) % 4, y)

    def zdev(d):
        return (((z + d + ZN) % ZN) * 2 + core, x, y)

    sib = (z * 2 + 1 - core, x, y)

    def src_of(d):
        return ((z + d + ZN) % ZN) * 2 + core

    def rep_of(sub):
        return (y - SUBS[sub] + 4) % 4

    loads = [
        pltpu.make_async_copy(u_hbm, u_ref, in_s.at[0]),
        pltpu.make_async_copy(lp_hbm, lp_ref, in_s.at[1]),
        pltpu.make_async_copy(piv_hbm, piv_ref, in_s.at[2]),
        pltpu.make_async_copy(ul_hbm, ul_ref, in_s.at[3]),
        pltpu.make_async_copy(
            ll_hbm.at[pl.ds(pl.multiple_of(x * 64, 64), 64)], ll_ref, in_s.at[4]
        ),
    ]
    for load in loads:
        load.start()
    bar = pltpu.get_barrier_semaphore()
    partners = [ydev(1), ydev(2), ydev(3), xdev(1), xdev(2), xdev(3), zdev(1), zdev(-1), sib]
    for p in partners:
        pl.semaphore_signal(bar, inc=1, device_id=p, device_id_type=MESH)

    def remote(src, dst, ss, rs, dev):
        return pltpu.make_async_remote_copy(
            src_ref=src, dst_ref=dst, send_sem=ss, recv_sem=rs, device_id=dev, device_id_type=MESH
        )

    def pack(ch):
        tile = 128 * (ch // 2)
        first = 64 * (ch % 2)
        parts = [
            u_ref[:, :, j, :, tile : tile + 128].reshape(2 * GROUPS * 16, 128) for j in range(GS)
        ]
        for yy in range(4):
            at = first + W * yy
            piece = jnp.concatenate([p[:, at : at + W] for p in parts], axis=1)
            pk[ch, yy] = piece.reshape(2, GROUPS, 16, 128)
        ug[ch, row, 0] = pk[ch, y]

    def a2a(ch, sub, receive=False):
        d = SUBS[sub]
        sems = (a2a_s.at[ch, sub - 1], a2a_r.at[ch, sub - 1], ydev(d))
        ref = ug.at[ch, row, sub]
        return remote(ref if receive else pk.at[ch, (y + d) % 4], ref, *sems)

    def ring(ch, way, step, half, receive=False):
        sign = 1 if way == 0 else -1
        origin = src_of(-sign * (step + 1 if receive else step))
        ref = ug.at[ch, origin, pl.ds(2 * half, 2)]
        return remote(
            ref, ref, ring_s.at[ch, way, step, half], ring_r.at[ch, way, step, half], zdev(sign)
        )

    def sibling(ch, d, receive=False):
        s = (z + d + ZN) % ZN
        ref = ug.at[ch, s * 2 + (1 - core if receive else core)]
        return remote(ref, ref, sib_s.at[ch, d % ZN], sib_r.at[ch, d % ZN], sib)

    def goes(way, step, half):
        return step < 3 or half == way

    def ring_step(ch, step):
        for half in range(2):
            if step == 0:
                for sub in (1,) if half == 0 else (2, 3):
                    a2a(ch, sub, True).wait_recv()
            for way in range(2):
                if step and goes(way, step - 1, half):
                    ring(ch, way, step - 1, half, True).wait_recv()
                if step < 4 and goes(way, step, half):
                    ring(ch, way, step, half).start()
        if step in (0, 4):
            sibling(ch, step).start()
        else:
            sibling(ch, -step).start()
            sibling(ch, step).start()

    def wait_sibling(ch):
        for d in range(ZN):
            sibling(ch, d, True).wait_recv()

    def a_first(d, receive=False):
        ref = la.at[0, (x - d + 4) % 4 if receive else x, pl.ds(0, 2)]
        return remote(ref, ref, a1_s.at[d - 1], a1_r.at[d - 1], xdev(d))

    def a_next(e, sub, receive=False):
        xx = (x - e + 4) % 4
        dst = la.at[sub, xx, pl.ds(0, 2)]
        src = dst if receive else la.at[0, xx, pl.ds(0, 2)]
        return remote(src, dst, a2_s.at[e, sub - 1], a2_r.at[e, sub - 1], ydev(SUBS[sub]))

    def b_first(sub, receive=False):
        dst = lb.at[sub, x, pl.ds(0, 3)]
        src = dst if receive else lb.at[0, x, pl.ds(0, 3)]
        return remote(src, dst, b1_s.at[sub - 1], b1_r.at[sub - 1], ydev(SUBS[sub]))

    def b_next(sub, d, receive=False):
        ref = lb.at[sub, (x - d + 4) % 4 if receive else x, pl.ds(0, 3)]
        return remote(ref, ref, b2_s.at[sub, d - 1], b2_r.at[sub, d - 1], xdev(d))

    def ship(ch, d, receive=False):
        dst = out_ref.at[ch, (y - d + 4) % 4 if receive else y]
        src = dst if receive else snd.at[ch, (y + d) % 4]
        return remote(src, dst, shp_s.at[ch, d - 1], shp_r.at[ch, d - 1], ydev(d))

    def lower_prep():
        first = jnp.dot(
            lp_ref[0].reshape(128, B), piv_ref[0], preferred_element_type=jnp.float32
        ).astype(jnp.bfloat16)
        la[0, x, 0:2] = first.reshape(2, 64, B)
        for d in (1, 3, 2):
            a_first(d).start()
        link = jnp.dot(ll_ref[...], piv_ref[0], preferred_element_type=jnp.float32)
        lb[0, x, 2] = link.astype(jnp.bfloat16)
        wide = first.astype(jnp.float32)
        pieces = []
        for g in range(2):
            sg = tab_ref[12, 4 * y + 2 + g]
            hit0 = jnp.where((sg >= 0) & (sg == tab_ref[12, 4 * y]), 1.0, 0.0)
            hit1 = jnp.where((sg >= 0) & (sg == tab_ref[12, 4 * y + 1]), 1.0, 0.0)
            pieces.append(wide[:64] * hit0 + wide[64:] * hit1)
        carried = jnp.concatenate(pieces, axis=0).astype(jnp.bfloat16)
        term = jnp.dot(carried, ul_ref[...], preferred_element_type=jnp.float32)
        diff = (lp_ref[1].reshape(128, B).astype(jnp.float32) - term).astype(jnp.bfloat16)
        second = jnp.dot(diff, piv_ref[1], preferred_element_type=jnp.float32).astype(jnp.bfloat16)
        lb[0, x, 0:2] = second.reshape(2, 64, B)
        for sub in (1, 2, 3):
            b_first(sub).start()

    def lower_forward():
        for d in (1, 3, 2):
            b_next(0, d).start()
        for sub in (1, 2, 3):
            a_next(0, sub).start()
        for i in range(3):
            sub, e = i + 1, (1, 3, 2)[i]
            b_first(sub, True).wait_recv()
            for d in (1, 3, 2):
                b_next(sub, d).start()
            a_first(e, True).wait_recv()
            for s in (1, 2, 3):
                a_next(e, s).start()

    def lower_select():
        for e in range(4):
            for s in (1, 2, 3):
                a_next(e, s, True).wait_recv()
        for s in range(4):
            for d in (1, 2, 3):
                b_next(s, d, True).wait_recv()
        for s in range(4):
            q = rep_of(s)
            for k, store in ((0, la), (1, lb)):
                s0 = tab_ref[12, 4 * q + 2 * k]
                s1 = tab_ref[12, 4 * q + 2 * k + 1]
                for a in range(2):
                    at = jnp.where(s0 == a, 0, jnp.where(s1 == a, 1, 2 + k))
                    for xx in range(4):
                        lsel[a, xx * 64 : xx * 64 + 64, (2 * s + k) * B : (2 * s + k + 1) * B] = (
                            store[s, xx, at]
                        )

    def turn(ch):
        def step(i, carry):
            s, k = i // 2, i % 2
            for g in range(GROUPS):
                block = ug[ch, :, s, k, g].reshape(B, 128)
                ut[s, k, GS * g : GS * g + GS] = block.T.reshape(GS, W, B)
            return carry

        lax.fori_loop(0, 8, step, 0)

    def arrange():
        def step(b, carry):
            rows = pl.ds(pl.multiple_of(b * W, W), W)
            for s in range(4):
                q = rep_of(s)
                lhs[rows, 2 * s * B : 2 * s * B + B] = ut[s, 0, tab_ref[q * 3, b]]
                lhs[rows, (2 * s + 1) * B : (2 * s + 2) * B] = ut[s, 1, tab_ref[q * 3 + 1, b]]
                acb[s, rows, :] = ut[s, 0, tab_ref[q * 3 + 2, b]]
            return carry

        lax.fori_loop(0, 32, step, 0)

    def second_upper():
        for s in range(4):
            link = lb[s, :, 2].reshape(B, B)
            shift = lax.dot_general(acb[s], link, NT, preferred_element_type=jnp.float32)
            cols = slice((2 * s + 1) * B, (2 * s + 2) * B)
            lhs[:, cols] = (lhs[:, cols].astype(jnp.float32) - shift).astype(jnp.bfloat16)

    def multiply():
        for a in range(2):
            prod = lax.dot_general(lhs[...], lsel[a], NT, preferred_element_type=jnp.float32)
            ctb[a] = prod.astype(jnp.bfloat16).reshape(32, W, B)

    def choose(ch):
        def step(i, carry):
            for j in range(4):
                e = tab_ref[13 + i // 8, (i % 8) * 4 + j]
                snd[ch, i // 4, (i % 4) * 4 + j] = ctb[e // 32, e % 32]
            return carry

        lax.fori_loop(0, 16, step, 0)

    def local_out(ch):
        return pltpu.make_async_copy(snd.at[ch, y], out_ref.at[ch, y], loc_s.at[ch])

    def p1(ch):
        wait_sibling(ch)
        turn(ch)

    def p2():
        arrange()
        second_upper()

    def p4(ch):
        choose(ch)
        for d in (1, 3, 2):
            ship(ch, d).start()
        local_out(ch).start()

    for s in range(4):
        for k in range(2):
            ut[s, k, SLOTS] = jnp.zeros((W, B), jnp.bfloat16)
        for xx in range(4):
            la[s, xx, 2] = jnp.zeros((64, B), jnp.bfloat16)
            lb[s, xx, 3] = jnp.zeros((64, B), jnp.bfloat16)
    loads[0].wait()
    pack(0)
    pl.semaphore_wait(bar, len(partners))
    for sub in (1, 2, 3):
        a2a(0, sub).start()
    pack(1)
    for sub in (1, 2, 3):
        a2a(1, sub).start()
    for load in loads[1:]:
        load.wait()
    lower_prep()
    ring_step(0, 0)
    for ch in (2, 3):
        pack(ch)
        for sub in (1, 2, 3):
            a2a(ch, sub).start()
        if ch == 2:
            ring_step(0, 1)
    ring_step(1, 0)
    lower_forward()
    ring_step(0, 2)
    ring_step(1, 1)
    ring_step(0, 3)
    ring_step(2, 0)
    ring_step(0, 4)
    ring_step(1, 2)
    p1(0)
    ring_step(2, 1)
    lower_select()
    p2()
    ring_step(1, 3)
    multiply()
    ring_step(3, 0)
    p4(0)
    ring_step(1, 4)
    ring_step(2, 2)
    p1(1)
    ring_step(3, 1)
    p2()
    ring_step(2, 3)
    multiply()
    ring_step(3, 2)
    p4(1)
    ring_step(2, 4)
    ring_step(3, 3)
    p1(2)
    p2()
    ring_step(3, 4)
    multiply()
    p4(2)
    p1(3)
    p2()
    multiply()
    p4(3)

    for ch in range(CH):
        for sub in (1, 2, 3):
            a2a(ch, sub).wait_send()
        for way in range(2):
            for step in range(4):
                for half in range(2):
                    if goes(way, step, half):
                        ring(ch, way, step, half).wait_send()
        for d in range(ZN):
            sibling(ch, d).wait_send()
    for i in range(4):
        for d in (1, 2, 3):
            a_next(i, d).wait_send()
            b_next(i, d).wait_send()
            if i == 0:
                a_first(d).wait_send()
                b_first(d).wait_send()
    for ch in range(CH):
        local_out(ch).wait()
        for d in (1, 2, 3):
            ship(ch, d).wait_send()
            ship(ch, d, True).wait_recv()


def finish_kernel(front_hbm, got_hbm, out_hbm, front, got, out, front_s, got_s, out_s):
    got_copies = [
        pltpu.make_async_copy(
            got_hbm.at[:, :, pl.ds(4 * i, 4)], got.at[:, :, pl.ds(4 * i, 4)], got_s.at[i]
        )
        for i in range(4)
    ]

    def fetch(i):
        return pltpu.make_async_copy(front_hbm.at[i], front.at[i], front_s.at[i])

    def store(i):
        return pltpu.make_async_copy(out.at[i], out_hbm.at[i], out_s.at[i])

    for i in range(16):
        if i % 4 == 0:
            got_copies[i // 4].start()
        fetch(i).start()
    for i in range(16):
        if i % 4 == 0:
            got_copies[i // 4].wait()
        fetch(i).wait()
        block = got[:, :, i].reshape(B, B)
        out[i] = front[i] - block.T.astype(jnp.float32)
        store(i).start()
    for i in range(16):
        store(i).wait()


def body(
    front,
    pivots,
    upper_link,
    lower_link,
    lower_panels,
    upper_panels,
    lower_slots,
    upper_slots,
    owner_map,
):
    names = jnp.arange(32, dtype=jnp.int32)
    same = upper_slots[:, :, None, :] == names[None, None, :, None]
    at = jnp.arange(SLOTS, dtype=jnp.int32)
    inv = jnp.min(jnp.where(same, at[None, None, None, :], SLOTS), axis=-1)
    carried = jnp.where(inv[:, 1] < SLOTS, inv[:, 0], SLOTS)
    inv = jnp.concatenate([inv, carried[:, None]], axis=1).reshape(12, 32)
    low = jnp.pad(lower_slots.reshape(1, 16), ((0, 0), (0, 16)))
    table = jnp.concatenate([inv, low, owner_map.reshape(2, 32)], axis=0)
    table = jnp.pad(table, ((0, TABLE - 15), (0, 0)))
    smem = pl.BlockSpec(memory_space=pltpu.SMEM)
    hbm = pl.BlockSpec(memory_space=pl.ANY)
    dma = pltpu.SemaphoreType.DMA
    bf = jnp.bfloat16
    got = pl.pallas_call(
        main_kernel,
        out_shape=jax.ShapeDtypeStruct((CH, 4, 16, W, B), bf),
        in_specs=[smem] + [hbm] * 5,
        out_specs=hbm,
        scratch_shapes=[
            pltpu.VMEM((2, GROUPS, GS, 16, B), bf),
            pltpu.VMEM((2, 2, 64, B), bf),
            pltpu.VMEM((2, B, B), bf),
            pltpu.VMEM((B, B), bf),
            pltpu.VMEM((64, B), bf),
            pltpu.VMEM((CH, 4, 2, GROUPS, 16, 128), bf),
            pltpu.VMEM((CH, 16, 4, 2, GROUPS, 16, 128), bf),
            pltpu.VMEM((4, 2, SLOTS + 1, W, B), bf),
            pltpu.VMEM((4, 4, 3, 64, B), bf),
            pltpu.VMEM((4, 4, 4, 64, B), bf),
            pltpu.VMEM((2, B, 8 * B), bf),
            pltpu.VMEM((32 * W, 8 * B), bf),
            pltpu.VMEM((4, 32 * W, B), bf),
            pltpu.VMEM((2, 32, W, B), bf),
            pltpu.VMEM((CH, 4, 16, W, B), bf),
            dma((5,)),
            dma((CH, 3)),
            dma((CH, 3)),
            dma((CH, 2, 4, 2)),
            dma((CH, 2, 4, 2)),
            dma((CH, ZN)),
            dma((CH, ZN)),
            dma((3,)),
            dma((3,)),
            dma((4, 3)),
            dma((4, 3)),
            dma((3,)),
            dma((3,)),
            dma((4, 3)),
            dma((4, 3)),
            dma((CH, 3)),
            dma((CH, 3)),
            dma((CH,)),
        ],
        compiler_params=pltpu.CompilerParams(
            collective_id=0, has_side_effects=True, vmem_limit_bytes=60 << 20
        ),
    )(
        table,
        upper_panels[0].reshape(2, GROUPS, GS, 16, B),
        lower_panels[0],
        pivots[0],
        upper_link[0],
        lower_link[0],
    )
    return pl.pallas_call(
        finish_kernel,
        out_shape=jax.ShapeDtypeStruct(front.shape, front.dtype),
        in_specs=[hbm, hbm],
        out_specs=hbm,
        scratch_shapes=[
            pltpu.VMEM((16, B, B), jnp.float32),
            pltpu.VMEM((CH, 4, 16, W, B), bf),
            pltpu.VMEM((16, B, B), jnp.float32),
            dma((16,)),
            dma((4,)),
            dma((16,)),
        ],
        compiler_params=pltpu.CompilerParams(vmem_limit_bytes=60 << 20),
    )(front, got)


def solution(mesh):
    return jax.shard_map(
        body,
        mesh=mesh,
        in_specs=(
            P(("row", "col", "rep"), None, None),
            P("rep", None, None, None),
            P("rep", None, None),
            P("rep", None, None),
            P("rep", None, "row", "col", None),
            P("rep", None, "col", "row", None),
            P(None, None, "row"),
            P(None, None, "col"),
            P(("row", "col"), None),
        ),
        out_specs=P(("row", "col", "rep"), None, None),
        check_vma=False,
    )
```

time: 99.4 us -> 79.9 us (0.80)
  Pallas kernels: 90.8 us -> 75.2 us
  local copies, waits for them, and re-layouts: 7.42 us -> 2.08 us
  other arithmetic: 0.81 us -> 2.14 us
    pallas_call x1, Pallas kernels: 83.5 us -> 70.7 us  [body(): pl.pallas_call(main_kernel, out_shape=jax.ShapeDtypeStruct((CH, 4, 16, W,...]
    unnamed x14 -> x2, local copies, waits for them, and re-layouts: 6.63 us -> 1.29 us
    pallas_call x1, Pallas kernels: 7.24 us -> 4.47 us  [body(): pl.pallas_call(finish_kernel, out_shape=jax.ShapeDtypeStruct(front.shape,...]
    unnamed x0 -> x1, other arithmetic: none -> 1.32 us
where the time goes in v2:
time: 79.9 us; the launch traced here: 79.4 us
  Pallas kernels  75.2 us (94%)
  other arithmetic  2.14 us (3%)
  local copies, waits for them, and re-layouts  2.08 us (3%)
    pallas_call x1, Pallas kernels, body(): pl.pallas_call(main_kernel, out_shape=jax.ShapeDtypeStruct((CH, 4, 16, W,...  70.7 us
    pallas_call x1, Pallas kernels, body(): pl.pallas_call(finish_kernel, out_shape=jax.ShapeDtypeStruct(front.shape,...  4.47 us

profile of v2, /device:TPU:1, one launch (start us, length us, event | category | flops | bytes accessed | tf_op | source)
XLA Modules:
  0.0 79.4 jit_solution(7162202625769862760)
XLA Ops:
  0.0 0.5 broadcast.10
  0.5 1.3 %reduce.3 = s32[64]{0:T(128)S(1)} reduce(s32[1,64]{1,0:T(1,128)} %param.17, s32[]{:T(128)} %broadcast.10), dimensions={0}, to_apply=%param.17.reduce_sub_computation.3 | reduce | bytes 516 | tf_op args[8]
  1.8 0.1 reshape.12
  1.9 0.8 %select_reduce_fusion = s32[4,2,32]{2,1,0:T(2,128)S(1)} fusion(s32[4,2,24]{2,1,0:T(2,128)} %param.16), kind=kLoop, calls=%fused_computation | loop fusion | flops 18176 | bytes 1792 | tf_op jit(solution)/shard_map/reduce_min | solution.py:430
  2.8 0.8 copy.12
  3.5 0.1 reshape.11
  3.6 0.6 pad.9.tab_ref
  4.2 70.7 %shard_map.91.got_hbm = bf16[4,4,16,16,256]{4,3,2,1,0:T(8,128)(2,1)} custom-call(s32[16,32]{1,0:T(8,128)} %pad.9.tab_ref, bf16[2,3,8,16,256]{4,3,2,1,0:T(8,128)(2,1)} %bitcast.5, bf16[2,2,64,256]{3,2,1,0:T(8,128)(2,1)} %bitcast.7, bf16[2,256,256]{2,1,0:T(8,128)(2,1)} %bitcast.6, bf16[256,256]{1,0:T(8,128)(2,1)} %bitcast.8, bf16[256,256]{1,0:T(8,128)(2,1)} %bitcast.9), custom_call_target="tpu_custom_call" | custom-call | tf_op jit(solution)/shard_map/pallas_call | solution.py:440
  75.0 4.5 %shard_map.92 = f32[16,256,256]{2,1,0:T(8,128)} custom-call(f32[16,256,256]{2,1,0:T(8,128)} %front_hbm.1, bf16[4,4,16,16,256]{4,3,2,1,0:T(8,128)(2,1)} %shard_map.91.got_hbm), custom_call_target="tpu_custom_call" | custom-call | tf_op jit(solution)/shard_map/pallas_call | solution.py:491
  (4 shorter events, 0.0 us)

commit v3 on v2

--- a/solution.py
+++ b/solution.py
@@ -13,13 +13,57 @@
 SLOTS = 24
 GS = 8
 GROUPS = 3
+PIECE = 2 * GROUPS * 16
 SUBS = (0, 1, 3, 2)
 ZN = 8
-TABLE = 16
+EVENTS = (
+    ("0", 0),
+    ("a2a", 2),
+    ("0", 1),
+    ("a2a", 3),
+    ("1", 0),
+    ("forward", 0),
+    ("1", 1),
+    ("2", 0),
+    ("0", 2),
+    ("2", 1),
+    ("3", 0),
+    ("1", 2),
+    ("4", 0),
+    ("0", 3),
+    ("p1", 0),
+    ("3", 1),
+    ("2", 2),
+    ("select", 0),
+    ("p2", 0),
+    ("4", 1),
+    ("1", 3),
+    ("p3", 0),
+    ("p4", 0),
+    ("3", 2),
+    ("p1", 1),
+    ("p2", 0),
+    ("2", 3),
+    ("p3", 0),
+    ("p4", 1),
+    ("4", 2),
+    ("3", 3),
+    ("p1", 2),
+    ("p2", 0),
+    ("4", 3),
+    ("p3", 0),
+    ("p4", 2),
+    ("p1", 3),
+    ("p2", 0),
+    ("p3", 0),
+    ("p4", 3),
+)
 
 
 def main_kernel(
     tab_ref,
+    low_ref,
+    own_ref,
     u_hbm,
     lp_hbm,
     piv_hbm,
@@ -48,6 +92,8 @@
     ring_r,
     sib_s,
     sib_r,
+    both_s,
+    both_r,
     a1_s,
     a1_r,
     a2_s,
@@ -96,6 +142,7 @@
         load.start()
     bar = pltpu.get_barrier_semaphore()
     partners = [ydev(1), ydev(2), ydev(3), xdev(1), xdev(2), xdev(3), zdev(1), zdev(-1), sib]
+    partners += [(((z + d + ZN) % ZN) * 2 + 1 - core, x, y) for d in (1, -1)]
     for p in partners:
         pl.semaphore_signal(bar, inc=1, device_id=p, device_id_type=MESH)
 
@@ -113,22 +160,33 @@
         for yy in range(4):
             at = first + W * yy
             piece = jnp.concatenate([p[:, at : at + W] for p in parts], axis=1)
-            pk[ch, yy] = piece.reshape(2, GROUPS, 16, 128)
-        ug[ch, row, 0] = pk[ch, y]
+            pk[ch, yy] = piece
+        ug[ch, row, 0:PIECE] = pk[ch, y]
 
     def a2a(ch, sub, receive=False):
         d = SUBS[sub]
         sems = (a2a_s.at[ch, sub - 1], a2a_r.at[ch, sub - 1], ydev(d))
-        ref = ug.at[ch, row, sub]
+        ref = ug.at[ch, row, pl.ds(sub * PIECE, PIECE)]
         return remote(ref if receive else pk.at[ch, (y + d) % 4], ref, *sems)
 
     def ring(ch, way, step, half, receive=False):
         sign = 1 if way == 0 else -1
         origin = src_of(-sign * (step + 1 if receive else step))
-        ref = ug.at[ch, origin, pl.ds(2 * half, 2)]
+        if step == 0:
+            ref = ug.at[ch, origin, pl.ds(half * PIECE, PIECE)]
+        else:
+            ref = ug.at[ch, origin, pl.ds(2 * half * PIECE, 2 * PIECE)]
         return remote(
             ref, ref, ring_s.at[ch, way, step, half], ring_r.at[ch, way, step, half], zdev(sign)
         )
+
+    def both(way, receive=False):
+        sign = 1 if way == 0 else -1
+        hops = -sign * (4 if receive else 3)
+        at = ((z + hops + ZN) % ZN) * 2 + (1 - core if receive else core)
+        ref = ug.at[CH - 1, at, pl.ds(2 * way * PIECE, 2 * PIECE)]
+        dev = (((z + sign + ZN) % ZN) * 2 + 1 - core, x, y)
+        return remote(ref, ref, both_s.at[way], both_r.at[way], dev)
 
     def sibling(ch, d, receive=False):
         s = (z + d + ZN) % ZN
@@ -138,25 +196,43 @@
     def goes(way, step, half):
         return step < 3 or half == way
 
+    def ring_own(ch):
+        for way in range(2):
+            ring(ch, way, 0, 0).start()
+
     def ring_step(ch, step):
+        if step == 0:
+            for sub in (1, 2, 3):
+                a2a(ch, sub, True).wait_recv()
+                for way in range(2):
+                    ring(ch, way, 0, sub).start()
+            sibling(ch, 0).start()
+            return
         for half in range(2):
-            if step == 0:
-                for sub in (1,) if half == 0 else (2, 3):
-                    a2a(ch, sub, True).wait_recv()
             for way in range(2):
-                if step and goes(way, step - 1, half):
+                if step == 1:
+                    ring(ch, way, 0, 2 * half, True).wait_recv()
+                    ring(ch, way, 0, 2 * half + 1, True).wait_recv()
+                elif goes(way, step - 1, half):
                     ring(ch, way, step - 1, half, True).wait_recv()
                 if step < 4 and goes(way, step, half):
                     ring(ch, way, step, half).start()
-        if step in (0, 4):
-            sibling(ch, step).start()
+                    if step == 3 and ch == CH - 1:
+                        both(way).start()
+        if step == 4:
+            if ch < CH - 1:
+                sibling(ch, step).start()
         else:
             sibling(ch, -step).start()
             sibling(ch, step).start()
 
     def wait_sibling(ch):
         for d in range(ZN):
-            sibling(ch, d, True).wait_recv()
+            if d == 4 and ch == CH - 1:
+                both(0, True).wait_recv()
+                both(1, True).wait_recv()
+            else:
+                sibling(ch, d, True).wait_recv()
 
     def a_first(d, receive=False):
         ref = la.at[0, (x - d + 4) % 4 if receive else x, pl.ds(0, 2)]
@@ -194,9 +270,9 @@
         wide = first.astype(jnp.float32)
         pieces = []
         for g in range(2):
-            sg = tab_ref[12, 4 * y + 2 + g]
-            hit0 = jnp.where((sg >= 0) & (sg == tab_ref[12, 4 * y]), 1.0, 0.0)
-            hit1 = jnp.where((sg >= 0) & (sg == tab_ref[12, 4 * y + 1]), 1.0, 0.0)
+            sg = low_ref[2 + g, y]
+            hit0 = jnp.where((sg >= 0) & (sg == low_ref[0, y]), 1.0, 0.0)
+            hit1 = jnp.where((sg >= 0) & (sg == low_ref[1, y]), 1.0, 0.0)
             pieces.append(wide[:64] * hit0 + wide[64:] * hit1)
         carried = jnp.concatenate(pieces, axis=0).astype(jnp.bfloat16)
         term = jnp.dot(carried, ul_ref[...], preferred_element_type=jnp.float32)
@@ -230,8 +306,8 @@
         for s in range(4):
             q = rep_of(s)
             for k, store in ((0, la), (1, lb)):
-                s0 = tab_ref[12, 4 * q + 2 * k]
-                s1 = tab_ref[12, 4 * q + 2 * k + 1]
+                s0 = low_ref[2 * k, q]
+                s1 = low_ref[2 * k + 1, q]
                 for a in range(2):
                     at = jnp.where(s0 == a, 0, jnp.where(s1 == a, 1, 2 + k))
                     for xx in range(4):
@@ -243,7 +319,8 @@
         def step(i, carry):
             s, k = i // 2, i % 2
             for g in range(GROUPS):
-                block = ug[ch, :, s, k, g].reshape(B, 128)
+                rows = pl.ds(pl.multiple_of((i * GROUPS + g) * 16, 16), 16)
+                block = ug[ch, :, rows, :].reshape(B, 128)
                 ut[s, k, GS * g : GS * g + GS] = block.T.reshape(GS, W, B)
             return carry
 
@@ -271,13 +348,14 @@
     def multiply():
         for a in range(2):
             prod = lax.dot_general(lhs[...], lsel[a], NT, preferred_element_type=jnp.float32)
-            ctb[a] = prod.astype(jnp.bfloat16).reshape(32, W, B)
+            ctb[32 * a : 32 * a + 32] = prod.astype(jnp.bfloat16).reshape(32, W, B)
 
     def choose(ch):
         def step(i, carry):
             for j in range(4):
-                e = tab_ref[13 + i // 8, (i % 8) * 4 + j]
-                snd[ch, i // 4, (i % 4) * 4 + j] = ctb[e // 32, e % 32]
+                e = own_ref[0, i * 4 + j]
+                rows = pl.ds(pl.multiple_of(((i % 4) * 4 + j) * W, W), W)
+                snd[ch, i // 4, rows, :] = ctb[e]
             return carry
 
         lax.fori_loop(0, 16, step, 0)
@@ -299,77 +377,65 @@
             ship(ch, d).start()
         local_out(ch).start()
 
-    for s in range(4):
-        for k in range(2):
-            ut[s, k, SLOTS] = jnp.zeros((W, B), jnp.bfloat16)
-        for xx in range(4):
-            la[s, xx, 2] = jnp.zeros((64, B), jnp.bfloat16)
-            lb[s, xx, 3] = jnp.zeros((64, B), jnp.bfloat16)
+    def zero_fill():
+        for s in range(4):
+            for k in range(2):
+                ut[s, k, SLOTS] = jnp.zeros((W, B), jnp.bfloat16)
+            for xx in range(4):
+                la[s, xx, 2] = jnp.zeros((64, B), jnp.bfloat16)
+                lb[s, xx, 3] = jnp.zeros((64, B), jnp.bfloat16)
+
+    def a2a_start(ch):
+        for sub in (1, 2, 3):
+            a2a(ch, sub).start()
+
     loads[0].wait()
     pack(0)
     pl.semaphore_wait(bar, len(partners))
-    for sub in (1, 2, 3):
-        a2a(0, sub).start()
+    a2a_start(0)
+    ring_own(0)
     pack(1)
-    for sub in (1, 2, 3):
-        a2a(1, sub).start()
+    a2a_start(1)
+    ring_own(1)
+    for ch in (2, 3):
+        pack(ch)
+        ring_own(ch)
     for load in loads[1:]:
         load.wait()
     lower_prep()
-    ring_step(0, 0)
-    for ch in (2, 3):
-        pack(ch)
-        for sub in (1, 2, 3):
-            a2a(ch, sub).start()
-        if ch == 2:
-            ring_step(0, 1)
-    ring_step(1, 0)
-    lower_forward()
-    ring_step(0, 2)
-    ring_step(1, 1)
-    ring_step(0, 3)
-    ring_step(2, 0)
-    ring_step(0, 4)
-    ring_step(1, 2)
-    p1(0)
-    ring_step(2, 1)
-    lower_select()
-    p2()
-    ring_step(1, 3)
-    multiply()
-    ring_step(3, 0)
-    p4(0)
-    ring_step(1, 4)
-    ring_step(2, 2)
-    p1(1)
-    ring_step(3, 1)
-    p2()
-    ring_step(2, 3)
-    multiply()
-    ring_step(3, 2)
-    p4(1)
-    ring_step(2, 4)
-    ring_step(3, 3)
-    p1(2)
-    p2()
-    ring_step(3, 4)
-    multiply()
-    p4(2)
-    p1(3)
-    p2()
-    multiply()
-    p4(3)
+    for what, ch in EVENTS:
+        if what == "a2a":
+            a2a_start(ch)
+        elif what == "forward":
+            zero_fill()
+            lower_forward()
+        elif what == "select":
+            lower_select()
+        elif what == "p1":
+            p1(ch)
+        elif what == "p2":
+            p2()
+        elif what == "p3":
+            multiply()
+        elif what == "p4":
+            p4(ch)
+        else:
+            ring_step(ch, int(what))
 
     for ch in range(CH):
         for sub in (1, 2, 3):
             a2a(ch, sub).wait_send()
         for way in range(2):
             for step in range(4):
-                for half in range(2):
+                for half in range(2 if step else 4):
                     if goes(way, step, half):
                         ring(ch, way, step, half).wait_send()
         for d in range(ZN):
-            sibling(ch, d).wait_send()
+            if d == 4 and ch == CH - 1:
+                both(0).wait_send()
+                both(1).wait_send()
+            else:
+                sibling(ch, d).wait_send()
     for i in range(4):
         for d in (1, 2, 3):
             a_next(i, d).wait_send()
@@ -387,7 +453,9 @@
 def finish_kernel(front_hbm, got_hbm, out_hbm, front, got, out, front_s, got_s, out_s):
     got_copies = [
         pltpu.make_async_copy(
-            got_hbm.at[:, :, pl.ds(4 * i, 4)], got.at[:, :, pl.ds(4 * i, 4)], got_s.at[i]
+            got_hbm.at[:, :, pl.ds(4 * W * i, 4 * W)],
+            got.at[:, :, pl.ds(4 * W * i, 4 * W)],
+            got_s.at[i],
         )
         for i in range(4)
     ]
@@ -406,7 +474,7 @@
         if i % 4 == 0:
             got_copies[i // 4].wait()
         fetch(i).wait()
-        block = got[:, :, i].reshape(B, B)
+        block = got[:, :, W * i : W * i + W].reshape(B, B)
         out[i] = front[i] - block.T.astype(jnp.float32)
         store(i).start()
     for i in range(16):
@@ -430,17 +498,14 @@
     inv = jnp.min(jnp.where(same, at[None, None, None, :], SLOTS), axis=-1)
     carried = jnp.where(inv[:, 1] < SLOTS, inv[:, 0], SLOTS)
     inv = jnp.concatenate([inv, carried[:, None]], axis=1).reshape(12, 32)
-    low = jnp.pad(lower_slots.reshape(1, 16), ((0, 0), (0, 16)))
-    table = jnp.concatenate([inv, low, owner_map.reshape(2, 32)], axis=0)
-    table = jnp.pad(table, ((0, TABLE - 15), (0, 0)))
     smem = pl.BlockSpec(memory_space=pltpu.SMEM)
     hbm = pl.BlockSpec(memory_space=pl.ANY)
     dma = pltpu.SemaphoreType.DMA
     bf = jnp.bfloat16
     got = pl.pallas_call(
         main_kernel,
-        out_shape=jax.ShapeDtypeStruct((CH, 4, 16, W, B), bf),
-        in_specs=[smem] + [hbm] * 5,
+        out_shape=jax.ShapeDtypeStruct((CH, 4, 16 * W, B), bf),
+        in_specs=[smem] * 3 + [hbm] * 5,
         out_specs=hbm,
         scratch_shapes=[
             pltpu.VMEM((2, GROUPS, GS, 16, B), bf),
@@ -448,23 +513,25 @@
             pltpu.VMEM((2, B, B), bf),
             pltpu.VMEM((B, B), bf),
             pltpu.VMEM((64, B), bf),
-            pltpu.VMEM((CH, 4, 2, GROUPS, 16, 128), bf),
-            pltpu.VMEM((CH, 16, 4, 2, GROUPS, 16, 128), bf),
+            pltpu.VMEM((CH, 4, PIECE, 128), bf),
+            pltpu.VMEM((CH, 16, 4 * PIECE, 128), bf),
             pltpu.VMEM((4, 2, SLOTS + 1, W, B), bf),
             pltpu.VMEM((4, 4, 3, 64, B), bf),
             pltpu.VMEM((4, 4, 4, 64, B), bf),
             pltpu.VMEM((2, B, 8 * B), bf),
             pltpu.VMEM((32 * W, 8 * B), bf),
             pltpu.VMEM((4, 32 * W, B), bf),
-            pltpu.VMEM((2, 32, W, B), bf),
-            pltpu.VMEM((CH, 4, 16, W, B), bf),
+            pltpu.VMEM((64, W, B), bf),
+            pltpu.VMEM((CH, 4, 16 * W, B), bf),
             dma((5,)),
             dma((CH, 3)),
             dma((CH, 3)),
-            dma((CH, 2, 4, 2)),
-            dma((CH, 2, 4, 2)),
+            dma((CH, 2, 4, 4)),
+            dma((CH, 2, 4, 4)),
             dma((CH, ZN)),
             dma((CH, ZN)),
+            dma((2,)),
+            dma((2,)),
             dma((3,)),
             dma((3,)),
             dma((4, 3)),
@@ -481,7 +548,9 @@
             collective_id=0, has_side_effects=True, vmem_limit_bytes=60 << 20
         ),
     )(
-        table,
+        inv,
+        jnp.transpose(lower_slots, (1, 2, 0)).reshape(4, 4),
+        owner_map,
         upper_panels[0].reshape(2, GROUPS, GS, 16, B),
         lower_panels[0],
         pivots[0],
@@ -495,7 +564,7 @@
         out_specs=hbm,
         scratch_shapes=[
             pltpu.VMEM((16, B, B), jnp.float32),
-            pltpu.VMEM((CH, 4, 16, W, B), bf),
+            pltpu.VMEM((CH, 4, 16 * W, B), bf),
             pltpu.VMEM((16, B, B), jnp.float32),
             dma((16,)),
             dma((4,)),

time: 79.9 us -> 72.1 us (0.902)
  Pallas kernels: 75.2 us -> 69.9 us
  local copies, waits for them, and re-layouts: 2.08 us -> 0.61 us
  other arithmetic: 2.14 us -> 0.81 us
    pallas_call x1, Pallas kernels: 70.7 us -> 65.4 us  [body(): pl.pallas_call(main_kernel, out_shape=jax.ShapeDtypeStruct((CH, 4, 16 * W...]
    unnamed x1 -> x0, other arithmetic: 1.32 us -> none
    unnamed x2 -> x0, local copies, waits for them, and re-layouts: 1.29 us -> none
where the time goes in v3:
time: 72.1 us; the launch traced here: 71.3 us
  Pallas kernels  69.9 us (97%)
  other arithmetic  0.81 us (1%)
    pallas_call x1, Pallas kernels, body(): pl.pallas_call(main_kernel, out_shape=jax.ShapeDtypeStruct((CH, 4, 16 * W...  65.4 us
    pallas_call x1, Pallas kernels, body(): pl.pallas_call(finish_kernel, out_shape=jax.ShapeDtypeStruct(front.shape,...  4.47 us

profile of v3, /device:TPU:1, one launch (start us, length us, event | category | flops | bytes accessed | tf_op | source)
XLA Modules:
  0.0 71.3 jit_solution(8189898927036497530)
XLA Ops:
  0.0 0.8 %select_reduce_fusion = s32[4,2,32]{2,1,0:T(2,128)S(1)} fusion(s32[4,2,24]{2,1,0:T(2,128)} %param.16), kind=kLoop, calls=%fused_computation | loop fusion | flops 18176 | bytes 1792 | tf_op jit(solution)/shard_map/reduce_min | solution.py:498
  0.8 0.6 reshape.7.tab_ref
  1.4 65.4 %shard_map.91.got_hbm = bf16[4,4,256,256]{3,2,1,0:T(8,128)(2,1)} custom-call(s32[12,32]{1,0:T(8,128)} %reshape.7.tab_ref, s32[4,4]{1,0:T(4,128)} %bitcast.13, s32[1,64]{1,0:T(1,128)} %own_ref.1, bf16[2,3,8,16,256]{4,3,2,1,0:T(8,128)(2,1)} %bitcast.8, bf16[2,2,64,256]{3,2,1,0:T(8,128)(2,1)} %bitcast.10, bf16[2,256,256]{2,1,0:T(8,128)(2,1)} %bitcast.9, ...), custom_call_target="tpu_custom_call" | custom-call | tf_op jit(solution)/shard_map/pallas_call | solution.py:505
  66.9 4.5 %shard_map.92 = f32[16,256,256]{2,1,0:T(8,128)} custom-call(f32[16,256,256]{2,1,0:T(8,128)} %front_hbm.1, bf16[4,4,256,256]{3,2,1,0:T(8,128)(2,1)} %shard_map.91.got_hbm), custom_call_target="tpu_custom_call" | custom-call | tf_op jit(solution)/shard_map/pallas_call | solution.py:560
  (2 shorter events, 0.0 us)

commit v4 on v3

--- a/solution.py
+++ b/solution.py
@@ -22,8 +22,8 @@
     ("0", 1),
     ("a2a", 3),
     ("1", 0),
+    ("1", 1),
     ("forward", 0),
-    ("1", 1),
     ("2", 0),
     ("0", 2),
     ("2", 1),
@@ -61,15 +61,18 @@
 
 
 def main_kernel(
-    tab_ref,
     low_ref,
     own_ref,
+    slots_hbm,
     u_hbm,
     lp_hbm,
     piv_hbm,
     ul_hbm,
     ll_hbm,
     out_ref,
+    slots_ref,
+    tab_vmem,
+    tab_ref,
     u_ref,
     lp_ref,
     piv_ref,
@@ -138,6 +141,7 @@
             ll_hbm.at[pl.ds(pl.multiple_of(x * 64, 64), 64)], ll_ref, in_s.at[4]
         ),
     ]
+    loads.append(pltpu.make_async_copy(slots_hbm, slots_ref, in_s.at[5]))
     for load in loads:
         load.start()
     bar = pltpu.get_barrier_semaphore()
@@ -281,12 +285,12 @@
         lb[0, x, 0:2] = second.reshape(2, 64, B)
         for sub in (1, 2, 3):
             b_first(sub).start()
-
-    def lower_forward():
+        for sub in (1, 2, 3):
+            a_next(0, sub).start()
         for d in (1, 3, 2):
             b_next(0, d).start()
-        for sub in (1, 2, 3):
-            a_next(0, sub).start()
+
+    def lower_forward():
         for i in range(3):
             sub, e = i + 1, (1, 3, 2)[i]
             b_first(sub, True).wait_recv()
@@ -316,24 +320,24 @@
                         )
 
     def turn(ch):
-        def step(i, carry):
-            s, k = i // 2, i % 2
-            for g in range(GROUPS):
-                rows = pl.ds(pl.multiple_of((i * GROUPS + g) * 16, 16), 16)
-                block = ug[ch, :, rows, :].reshape(B, 128)
-                ut[s, k, GS * g : GS * g + GS] = block.T.reshape(GS, W, B)
+        def step(s, carry):
+            for k in range(2):
+                for g in range(GROUPS):
+                    rows = pl.ds(pl.multiple_of(s * PIECE + (k * GROUPS + g) * 16, 16), 16)
+                    block = ug[ch, :, rows, :].reshape(B, 128)
+                    ut[s, k, GS * g : GS * g + GS] = block.T.reshape(GS, W, B)
             return carry
 
-        lax.fori_loop(0, 8, step, 0)
+        lax.fori_loop(0, 4, step, 0)
 
     def arrange():
         def step(b, carry):
             rows = pl.ds(pl.multiple_of(b * W, W), W)
             for s in range(4):
                 q = rep_of(s)
-                lhs[rows, 2 * s * B : 2 * s * B + B] = ut[s, 0, tab_ref[q * 3, b]]
-                lhs[rows, (2 * s + 1) * B : (2 * s + 2) * B] = ut[s, 1, tab_ref[q * 3 + 1, b]]
-                acb[s, rows, :] = ut[s, 0, tab_ref[q * 3 + 2, b]]
+                lhs[rows, 2 * s * B : 2 * s * B + B] = ut[s, 0, tab_ref[b, q * 3]]
+                lhs[rows, (2 * s + 1) * B : (2 * s + 2) * B] = ut[s, 1, tab_ref[b, q * 3 + 1]]
+                acb[s, rows, :] = ut[s, 0, tab_ref[b, q * 3 + 2]]
             return carry
 
         lax.fori_loop(0, 32, step, 0)
@@ -352,13 +356,11 @@
 
     def choose(ch):
         def step(i, carry):
-            for j in range(4):
-                e = own_ref[0, i * 4 + j]
-                rows = pl.ds(pl.multiple_of(((i % 4) * 4 + j) * W, W), W)
-                snd[ch, i // 4, rows, :] = ctb[e]
+            for j in range(16):
+                snd[ch, i, j * W : j * W + W, :] = ctb[own_ref[0, i * 16 + j]]
             return carry
 
-        lax.fori_loop(0, 16, step, 0)
+        lax.fori_loop(0, 4, step, 0)
 
     def local_out(ch):
         return pltpu.make_async_copy(snd.at[ch, y], out_ref.at[ch, y], loc_s.at[ch])
@@ -376,6 +378,26 @@
         for d in (1, 3, 2):
             ship(ch, d).start()
         local_out(ch).start()
+
+    def make_table():
+        column = lax.broadcasted_iota(jnp.int32, (32, 128), 1)
+        name = lax.broadcasted_iota(jnp.int32, (32, SLOTS), 0)
+        at = lax.broadcasted_iota(jnp.int32, (32, SLOTS), 1)
+        table = jnp.zeros((32, 128), jnp.int32)
+        for q in range(4):
+            found = [
+                jnp.min(
+                    jnp.where(slots_ref[q, k : k + 1, :] == name, at, SLOTS),
+                    axis=1,
+                    keepdims=True,
+                )
+                for k in range(2)
+            ]
+            found.append(jnp.where(found[1] < SLOTS, found[0], SLOTS))
+            for k in range(3):
+                table = jnp.where(column == 3 * q + k, found[k], table)
+        tab_vmem[...] = table
+        pltpu.make_async_copy(tab_vmem, tab_ref, in_s.at[6]).start()
 
     def zero_fill():
         for s in range(4):
@@ -409,8 +431,10 @@
         elif what == "forward":
             zero_fill()
             lower_forward()
+            make_table()
         elif what == "select":
             lower_select()
+            pltpu.make_async_copy(tab_vmem, tab_ref, in_s.at[6]).wait()
         elif what == "p1":
             p1(ch)
         elif what == "p2":
@@ -492,12 +516,6 @@
     upper_slots,
     owner_map,
 ):
-    names = jnp.arange(32, dtype=jnp.int32)
-    same = upper_slots[:, :, None, :] == names[None, None, :, None]
-    at = jnp.arange(SLOTS, dtype=jnp.int32)
-    inv = jnp.min(jnp.where(same, at[None, None, None, :], SLOTS), axis=-1)
-    carried = jnp.where(inv[:, 1] < SLOTS, inv[:, 0], SLOTS)
-    inv = jnp.concatenate([inv, carried[:, None]], axis=1).reshape(12, 32)
     smem = pl.BlockSpec(memory_space=pltpu.SMEM)
     hbm = pl.BlockSpec(memory_space=pl.ANY)
     dma = pltpu.SemaphoreType.DMA
@@ -505,9 +523,12 @@
     got = pl.pallas_call(
         main_kernel,
         out_shape=jax.ShapeDtypeStruct((CH, 4, 16 * W, B), bf),
-        in_specs=[smem] * 3 + [hbm] * 5,
+        in_specs=[smem] * 2 + [hbm] * 6,
         out_specs=hbm,
         scratch_shapes=[
+            pltpu.VMEM((4, 2, SLOTS), jnp.int32),
+            pltpu.VMEM((32, 128), jnp.int32),
+            pltpu.SMEM((32, 128), jnp.int32),
             pltpu.VMEM((2, GROUPS, GS, 16, B), bf),
             pltpu.VMEM((2, 2, 64, B), bf),
             pltpu.VMEM((2, B, B), bf),
@@ -523,7 +544,7 @@
             pltpu.VMEM((4, 32 * W, B), bf),
             pltpu.VMEM((64, W, B), bf),
             pltpu.VMEM((CH, 4, 16 * W, B), bf),
-            dma((5,)),
+            dma((7,)),
             dma((CH, 3)),
             dma((CH, 3)),
             dma((CH, 2, 4, 4)),
@@ -548,9 +569,9 @@
             collective_id=0, has_side_effects=True, vmem_limit_bytes=60 << 20
         ),
     )(
-        inv,
         jnp.transpose(lower_slots, (1, 2, 0)).reshape(4, 4),
         owner_map,
+        upper_slots,
         upper_panels[0].reshape(2, GROUPS, GS, 16, B),
         lower_panels[0],
         pivots[0],

time: 72.1 us -> 69.8 us (0.968)
  other arithmetic: 0.81 us -> 0 us
    reduce_min x1 -> x0, other arithmetic: 0.8 us -> none  [body(): inv = jnp.min(jnp.where(same, at[None, None, None, :], SLOTS), axis=-1)]
where the time goes in v4:
time: 69.8 us; the launch traced here: 69.7 us
  Pallas kernels  69.6 us (100%)
    pallas_call x1, Pallas kernels, body(): pl.pallas_call(main_kernel, out_shape=jax.ShapeDtypeStruct((CH, 4, 16 * W...  65.2 us
    pallas_call x1, Pallas kernels, body(): pl.pallas_call(finish_kernel, out_shape=jax.ShapeDtypeStruct(front.shape,...  4.47 us

profile of v4, /device:TPU:1, one launch (start us, length us, event | category | flops | bytes accessed | tf_op | source)
XLA Modules:
  0.0 69.7 jit_solution(17051451119422995385)
XLA Ops:
  0.0 65.2 %shard_map.91.got_hbm = bf16[4,4,256,256]{3,2,1,0:T(8,128)(2,1)} custom-call(s32[4,4]{1,0:T(4,128)} %bitcast.13, s32[1,64]{1,0:T(1,128)} %own_ref.1, s32[4,2,24]{2,1,0:T(2,128)} %slots_hbm.1, bf16[2,3,8,16,256]{4,3,2,1,0:T(8,128)(2,1)} %bitcast.8, bf16[2,2,64,256]{3,2,1,0:T(8,128)(2,1)} %bitcast.10, bf16[2,256,256]{2,1,0:T(8,128)(2,1)} %bitcast.9, ...), custom_call_target="tpu_custom_call" | custom-call | tf_op jit(solution)/shard_map/pallas_call | solution.py:523
  65.2 4.5 %shard_map.92 = f32[16,256,256]{2,1,0:T(8,128)} custom-call(f32[16,256,256]{2,1,0:T(8,128)} %front_hbm.1, bf16[4,4,256,256]{3,2,1,0:T(8,128)(2,1)} %shard_map.91.got_hbm), custom_call_target="tpu_custom_call" | custom-call | tf_op jit(solution)/shard_map/pallas_call | solution.py:581

commit v5 on v4

--- a/solution.py
+++ b/solution.py
@@ -93,10 +93,7 @@
     a2a_r,
     ring_s,
     ring_r,
-    sib_s,
     sib_r,
-    both_s,
-    both_r,
     a1_s,
     a1_r,
     a2_s,
@@ -169,33 +166,30 @@
 
     def a2a(ch, sub, receive=False):
         d = SUBS[sub]
-        sems = (a2a_s.at[ch, sub - 1], a2a_r.at[ch, sub - 1], ydev(d))
+        sems = (a2a_s.at[0], a2a_r.at[ch, sub - 1], ydev(d))
         ref = ug.at[ch, row, pl.ds(sub * PIECE, PIECE)]
         return remote(ref if receive else pk.at[ch, (y + d) % 4], ref, *sems)
 
-    def ring(ch, way, step, half, receive=False):
+    def ring(ch, way, step, part, receive=False):
         sign = 1 if way == 0 else -1
         origin = src_of(-sign * (step + 1 if receive else step))
-        if step == 0:
-            ref = ug.at[ch, origin, pl.ds(half * PIECE, PIECE)]
+        if step == 0 and not receive:
+            ref = ug.at[ch, origin, pl.ds(part * PIECE, PIECE)]
+            slot = part // 2
         else:
-            ref = ug.at[ch, origin, pl.ds(2 * half * PIECE, 2 * PIECE)]
-        return remote(
-            ref, ref, ring_s.at[ch, way, step, half], ring_r.at[ch, way, step, half], zdev(sign)
-        )
-
-    def both(way, receive=False):
+            ref = ug.at[ch, origin, pl.ds(2 * part * PIECE, 2 * PIECE)]
+            slot = 2 * step + part if step < 3 else 6
+        return remote(ref, ref, ring_s.at[ch], ring_r.at[ch, way, slot], zdev(sign))
+
+    def both(way):
         sign = 1 if way == 0 else -1
-        hops = -sign * (4 if receive else 3)
-        at = ((z + hops + ZN) % ZN) * 2 + (1 - core if receive else core)
-        ref = ug.at[CH - 1, at, pl.ds(2 * way * PIECE, 2 * PIECE)]
+        ref = ug.at[CH - 1, src_of(-3 * sign), pl.ds(2 * way * PIECE, 2 * PIECE)]
         dev = (((z + sign + ZN) % ZN) * 2 + 1 - core, x, y)
-        return remote(ref, ref, both_s.at[way], both_r.at[way], dev)
-
-    def sibling(ch, d, receive=False):
-        s = (z + d + ZN) % ZN
-        ref = ug.at[ch, s * 2 + (1 - core if receive else core)]
-        return remote(ref, ref, sib_s.at[ch, d % ZN], sib_r.at[ch, d % ZN], sib)
+        return remote(ref, ref, ring_s.at[CH - 1], sib_r.at[CH - 1], dev)
+
+    def sibling(ch, d):
+        ref = ug.at[ch, src_of(d)]
+        return remote(ref, ref, ring_s.at[ch], sib_r.at[ch], sib)
 
     def goes(way, step, half):
         return step < 3 or half == way
@@ -214,10 +208,7 @@
             return
         for half in range(2):
             for way in range(2):
-                if step == 1:
-                    ring(ch, way, 0, 2 * half, True).wait_recv()
-                    ring(ch, way, 0, 2 * half + 1, True).wait_recv()
-                elif goes(way, step - 1, half):
+                if goes(way, step - 1, half):
                     ring(ch, way, step - 1, half, True).wait_recv()
                 if step < 4 and goes(way, step, half):
                     ring(ch, way, step, half).start()
@@ -231,36 +222,32 @@
             sibling(ch, step).start()
 
     def wait_sibling(ch):
-        for d in range(ZN):
-            if d == 4 and ch == CH - 1:
-                both(0, True).wait_recv()
-                both(1, True).wait_recv()
-            else:
-                sibling(ch, d, True).wait_recv()
+        ref = ug.at[ch, pl.ds(0, ZN)]
+        remote(ref, ref, ring_s.at[ch], sib_r.at[ch], sib).wait_recv()
 
     def a_first(d, receive=False):
         ref = la.at[0, (x - d + 4) % 4 if receive else x, pl.ds(0, 2)]
-        return remote(ref, ref, a1_s.at[d - 1], a1_r.at[d - 1], xdev(d))
+        return remote(ref, ref, a1_s.at[0], a1_r.at[d - 1], xdev(d))
 
     def a_next(e, sub, receive=False):
         xx = (x - e + 4) % 4
         dst = la.at[sub, xx, pl.ds(0, 2)]
         src = dst if receive else la.at[0, xx, pl.ds(0, 2)]
-        return remote(src, dst, a2_s.at[e, sub - 1], a2_r.at[e, sub - 1], ydev(SUBS[sub]))
+        return remote(src, dst, a2_s.at[0], a2_r.at[0], ydev(SUBS[sub]))
 
     def b_first(sub, receive=False):
         dst = lb.at[sub, x, pl.ds(0, 3)]
         src = dst if receive else lb.at[0, x, pl.ds(0, 3)]
-        return remote(src, dst, b1_s.at[sub - 1], b1_r.at[sub - 1], ydev(SUBS[sub]))
+        return remote(src, dst, b1_s.at[0], b1_r.at[sub - 1], ydev(SUBS[sub]))
 
     def b_next(sub, d, receive=False):
         ref = lb.at[sub, (x - d + 4) % 4 if receive else x, pl.ds(0, 3)]
-        return remote(ref, ref, b2_s.at[sub, d - 1], b2_r.at[sub, d - 1], xdev(d))
+        return remote(ref, ref, b2_s.at[0], b2_r.at[0], xdev(d))
 
     def ship(ch, d, receive=False):
         dst = out_ref.at[ch, (y - d + 4) % 4 if receive else y]
         src = dst if receive else snd.at[ch, (y + d) % 4]
-        return remote(src, dst, shp_s.at[ch, d - 1], shp_r.at[ch, d - 1], ydev(d))
+        return remote(src, dst, shp_s.at[0], shp_r.at[0], ydev(d))
 
     def lower_prep():
         first = jnp.dot(
@@ -301,12 +288,10 @@
                 a_next(e, s).start()
 
     def lower_select():
-        for e in range(4):
-            for s in (1, 2, 3):
-                a_next(e, s, True).wait_recv()
-        for s in range(4):
-            for d in (1, 2, 3):
-                b_next(s, d, True).wait_recv()
+        ref = la.at[pl.ds(1, 3), :, pl.ds(0, 2)]
+        remote(ref, ref, a2_s.at[0], a2_r.at[0], ydev(1)).wait_recv()
+        ref = lb.at[pl.ds(0, 3), :, pl.ds(0, 3)]
+        remote(ref, ref, b2_s.at[0], b2_r.at[0], xdev(1)).wait_recv()
         for s in range(4):
             q = rep_of(s)
             for k, store in ((0, la), (1, lb)):
@@ -363,7 +348,7 @@
         lax.fori_loop(0, 4, step, 0)
 
     def local_out(ch):
-        return pltpu.make_async_copy(snd.at[ch, y], out_ref.at[ch, y], loc_s.at[ch])
+        return pltpu.make_async_copy(snd.at[ch, y], out_ref.at[ch, y], loc_s.at[0])
 
     def p1(ch):
         wait_sibling(ch)
@@ -446,32 +431,20 @@
         else:
             ring_step(ch, int(what))
 
+    def sent(ref, sem):
+        remote(ref, ref, sem, shp_r.at[0], sib).wait_send()
+
+    sent(ug.at[0, pl.ds(0, 3)], a2a_s.at[0])
     for ch in range(CH):
-        for sub in (1, 2, 3):
-            a2a(ch, sub).wait_send()
-        for way in range(2):
-            for step in range(4):
-                for half in range(2 if step else 4):
-                    if goes(way, step, half):
-                        ring(ch, way, step, half).wait_send()
-        for d in range(ZN):
-            if d == 4 and ch == CH - 1:
-                both(0).wait_send()
-                both(1).wait_send()
-            else:
-                sibling(ch, d).wait_send()
-    for i in range(4):
-        for d in (1, 2, 3):
-            a_next(i, d).wait_send()
-            b_next(i, d).wait_send()
-            if i == 0:
-                a_first(d).wait_send()
-                b_first(d).wait_send()
-    for ch in range(CH):
-        local_out(ch).wait()
-        for d in (1, 2, 3):
-            ship(ch, d).wait_send()
-            ship(ch, d, True).wait_recv()
+        sent(ug.at[ch, pl.ds(0, 15)], ring_s.at[ch])
+    sent(la.at[0, pl.ds(0, 3), pl.ds(0, 2)], a1_s.at[0])
+    sent(la.at[pl.ds(1, 3), :, pl.ds(0, 2)], a2_s.at[0])
+    sent(lb.at[0, pl.ds(0, 3), pl.ds(0, 3)], b1_s.at[0])
+    sent(lb.at[pl.ds(0, 3), :, pl.ds(0, 3)], b2_s.at[0])
+    sent(snd.at[pl.ds(0, 3)], shp_s.at[0])
+    pltpu.make_async_copy(snd.at[0], out_ref.at[0], loc_s.at[0]).wait()
+    ref = out_ref.at[pl.ds(0, 3)]
+    remote(ref, ref, shp_s.at[0], shp_r.at[0], ydev(1)).wait_recv()
 
 
 def finish_kernel(front_hbm, got_hbm, out_hbm, front, got, out, front_s, got_s, out_s):
@@ -545,25 +518,22 @@
             pltpu.VMEM((64, W, B), bf),
             pltpu.VMEM((CH, 4, 16 * W, B), bf),
             dma((7,)),
-            dma((CH, 3)),
-            dma((CH, 3)),
-            dma((CH, 2, 4, 4)),
-            dma((CH, 2, 4, 4)),
-            dma((CH, ZN)),
-            dma((CH, ZN)),
-            dma((2,)),
-            dma((2,)),
-            dma((3,)),
-            dma((3,)),
-            dma((4, 3)),
-            dma((4, 3)),
-            dma((3,)),
-            dma((3,)),
-            dma((4, 3)),
-            dma((4, 3)),
-            dma((CH, 3)),
+            dma((1,)),
             dma((CH, 3)),
             dma((CH,)),
+            dma((CH, 2, 7)),
+            dma((CH,)),
+            dma((1,)),
+            dma((3,)),
+            dma((1,)),
+            dma((1,)),
+            dma((1,)),
+            dma((3,)),
+            dma((1,)),
+            dma((1,)),
+            dma((1,)),
+            dma((1,)),
+            dma((1,)),
         ],
         compiler_params=pltpu.CompilerParams(
             collective_id=0, has_side_effects=True, vmem_limit_bytes=60 << 20

time: 69.8 us -> 66.7 us (0.956)
  Pallas kernels: 69.6 us -> 66.6 us
    pallas_call x1, Pallas kernels: 65.2 us -> 62.1 us  [body(): pl.pallas_call(main_kernel, out_shape=jax.ShapeDtypeStruct((CH, 4, 16 * W...]
where the time goes in v5:
time: 66.7 us; the launch traced here: 66.6 us
  Pallas kernels  66.6 us (100%)
    pallas_call x1, Pallas kernels, body(): pl.pallas_call(main_kernel, out_shape=jax.ShapeDtypeStruct((CH, 4, 16 * W...  62.1 us
    pallas_call x1, Pallas kernels, body(): pl.pallas_call(finish_kernel, out_shape=jax.ShapeDtypeStruct(front.shape,...  4.47 us

profile of v5, /device:TPU:1, one launch (start us, length us, event | category | flops | bytes accessed | tf_op | source)
XLA Modules:
  0.0 66.6 jit_solution(3873547591599968264)
XLA Ops:
  0.0 62.1 %shard_map.91.got_hbm = bf16[4,4,256,256]{3,2,1,0:T(8,128)(2,1)} custom-call(s32[4,4]{1,0:T(4,128)} %bitcast.13, s32[1,64]{1,0:T(1,128)} %own_ref.1, s32[4,2,24]{2,1,0:T(2,128)} %slots_hbm.1, bf16[2,3,8,16,256]{4,3,2,1,0:T(8,128)(2,1)} %bitcast.8, bf16[2,2,64,256]{3,2,1,0:T(8,128)(2,1)} %bitcast.10, bf16[2,256,256]{2,1,0:T(8,128)(2,1)} %bitcast.9, ...), custom_call_target="tpu_custom_call" | custom-call | tf_op jit(solution)/shard_map/pallas_call | solution.py:496
  62.1 4.5 %shard_map.92 = f32[16,256,256]{2,1,0:T(8,128)} custom-call(f32[16,256,256]{2,1,0:T(8,128)} %front_hbm.1, bf16[4,4,256,256]{3,2,1,0:T(8,128)(2,1)} %shard_map.91.got_hbm), custom_call_target="tpu_custom_call" | custom-call | tf_op jit(solution)/shard_map/pallas_call | solution.py:551

commit v6 on v5

--- a/solution.py
+++ b/solution.py
@@ -26,22 +26,22 @@
     ("forward", 0),
     ("2", 0),
     ("0", 2),
+    ("3", 0),
     ("2", 1),
-    ("3", 0),
+    ("4", 0),
     ("1", 2),
-    ("4", 0),
-    ("0", 3),
     ("p1", 0),
     ("3", 1),
-    ("2", 2),
+    ("0", 3),
     ("select", 0),
     ("p2", 0),
     ("4", 1),
-    ("1", 3),
+    ("2", 2),
     ("p3", 0),
     ("p4", 0),
+    ("1", 3),
+    ("p1", 1),
     ("3", 2),
-    ("p1", 1),
     ("p2", 0),
     ("2", 3),
     ("p3", 0),
@@ -50,9 +50,9 @@
     ("3", 3),
     ("p1", 2),
     ("p2", 0),
-    ("4", 3),
     ("p3", 0),
     ("p4", 2),
+    ("4", 3),
     ("p1", 3),
     ("p2", 0),
     ("p3", 0),
@@ -166,30 +166,38 @@
 
     def a2a(ch, sub, receive=False):
         d = SUBS[sub]
-        sems = (a2a_s.at[0], a2a_r.at[ch, sub - 1], ydev(d))
-        ref = ug.at[ch, row, pl.ds(sub * PIECE, PIECE)]
-        return remote(ref if receive else pk.at[ch, (y + d) % 4], ref, *sems)
+        sems = (a2a_s.at[0], a2a_r.at[ch], ydev(d))
+        if receive:
+            ref = ug.at[ch, row, pl.ds(PIECE, 3 * PIECE)]
+            return remote(ref, ref, *sems)
+        return remote(pk.at[ch, (y + d) % 4], ug.at[ch, row, pl.ds(sub * PIECE, PIECE)], *sems)
 
     def ring(ch, way, step, part, receive=False):
         sign = 1 if way == 0 else -1
         origin = src_of(-sign * (step + 1 if receive else step))
-        if step == 0 and not receive:
+        fine = ch == CH - 1
+        if fine or (step == 0 and not receive):
             ref = ug.at[ch, origin, pl.ds(part * PIECE, PIECE)]
+        else:
+            ref = ug.at[ch, origin, pl.ds(2 * part * PIECE, 2 * PIECE)]
+        if fine:
+            slot = 4 * step + part if step < 3 else 12 + part % 2
+        elif step == 0 and not receive:
             slot = part // 2
         else:
-            ref = ug.at[ch, origin, pl.ds(2 * part * PIECE, 2 * PIECE)]
             slot = 2 * step + part if step < 3 else 6
-        return remote(ref, ref, ring_s.at[ch], ring_r.at[ch, way, slot], zdev(sign))
-
-    def both(way):
+        sem = ring_r.at[ch + slot // 7, way, slot % 7]
+        return remote(ref, ref, ring_s.at[0], sem, zdev(sign))
+
+    def both(way, part):
         sign = 1 if way == 0 else -1
-        ref = ug.at[CH - 1, src_of(-3 * sign), pl.ds(2 * way * PIECE, 2 * PIECE)]
+        ref = ug.at[CH - 1, src_of(-3 * sign), pl.ds(part * PIECE, PIECE)]
         dev = (((z + sign + ZN) % ZN) * 2 + 1 - core, x, y)
-        return remote(ref, ref, ring_s.at[CH - 1], sib_r.at[CH - 1], dev)
+        return remote(ref, ref, ring_s.at[0], sib_r.at[CH - 1], dev)
 
     def sibling(ch, d):
         ref = ug.at[ch, src_of(d)]
-        return remote(ref, ref, ring_s.at[ch], sib_r.at[ch], sib)
+        return remote(ref, ref, ring_s.at[0], sib_r.at[ch], sib)
 
     def goes(way, step, half):
         return step < 3 or half == way
@@ -200,20 +208,22 @@
 
     def ring_step(ch, step):
         if step == 0:
+            a2a(ch, 1, True).wait_recv()
             for sub in (1, 2, 3):
-                a2a(ch, sub, True).wait_recv()
                 for way in range(2):
                     ring(ch, way, 0, sub).start()
             sibling(ch, 0).start()
             return
-        for half in range(2):
+        fine = ch == CH - 1
+        for part in range(4 if fine else 2):
+            half = part // 2 if fine else part
             for way in range(2):
                 if goes(way, step - 1, half):
-                    ring(ch, way, step - 1, half, True).wait_recv()
+                    ring(ch, way, step - 1, part, True).wait_recv()
                 if step < 4 and goes(way, step, half):
-                    ring(ch, way, step, half).start()
-                    if step == 3 and ch == CH - 1:
-                        both(way).start()
+                    ring(ch, way, step, part).start()
+                    if step == 3 and fine:
+                        both(way, part).start()
         if step == 4:
             if ch < CH - 1:
                 sibling(ch, step).start()
@@ -223,7 +233,7 @@
 
     def wait_sibling(ch):
         ref = ug.at[ch, pl.ds(0, ZN)]
-        remote(ref, ref, ring_s.at[ch], sib_r.at[ch], sib).wait_recv()
+        remote(ref, ref, ring_s.at[0], sib_r.at[ch], sib).wait_recv()
 
     def a_first(d, receive=False):
         ref = la.at[0, (x - d + 4) % 4 if receive else x, pl.ds(0, 2)]
@@ -435,8 +445,7 @@
         remote(ref, ref, sem, shp_r.at[0], sib).wait_send()
 
     sent(ug.at[0, pl.ds(0, 3)], a2a_s.at[0])
-    for ch in range(CH):
-        sent(ug.at[ch, pl.ds(0, 15)], ring_s.at[ch])
+    sent(ug.at[:, pl.ds(0, 15)], ring_s.at[0])
     sent(la.at[0, pl.ds(0, 3), pl.ds(0, 2)], a1_s.at[0])
     sent(la.at[pl.ds(1, 3), :, pl.ds(0, 2)], a2_s.at[0])
     sent(lb.at[0, pl.ds(0, 3), pl.ds(0, 3)], b1_s.at[0])
@@ -461,7 +470,7 @@
         return pltpu.make_async_copy(front_hbm.at[i], front.at[i], front_s.at[i])
 
     def store(i):
-        return pltpu.make_async_copy(out.at[i], out_hbm.at[i], out_s.at[i])
+        return pltpu.make_async_copy(out.at[i], out_hbm.at[i], out_s.at[0])
 
     for i in range(16):
         if i % 4 == 0:
@@ -474,8 +483,7 @@
         block = got[:, :, W * i : W * i + W].reshape(B, B)
         out[i] = front[i] - block.T.astype(jnp.float32)
         store(i).start()
-    for i in range(16):
-        store(i).wait()
+    pltpu.make_async_copy(out, out_hbm, out_s.at[0]).wait()
 
 
 def body(
@@ -519,9 +527,9 @@
             pltpu.VMEM((CH, 4, 16 * W, B), bf),
             dma((7,)),
             dma((1,)),
-            dma((CH, 3)),
             dma((CH,)),
-            dma((CH, 2, 7)),
+            dma((1,)),
+            dma((CH + 1, 2, 7)),
             dma((CH,)),
             dma((1,)),
             dma((3,)),
@@ -559,7 +567,7 @@
             pltpu.VMEM((16, B, B), jnp.float32),
             dma((16,)),
             dma((4,)),
-            dma((16,)),
+            dma((1,)),
         ],
         compiler_params=pltpu.CompilerParams(vmem_limit_bytes=60 << 20),
     )(front, got)

time: 66.7 us -> 66.7 us (level)
  Pallas kernels: 66.6 us -> 65.9 us
where the time goes in v6:
time: 66.7 us; the launch traced here: 65.9 us
  Pallas kernels  65.9 us (99%)
    pallas_call x1, Pallas kernels, body(): pl.pallas_call(main_kernel, out_shape=jax.ShapeDtypeStruct((CH, 4, 16 * W...  61.6 us
    pallas_call x1, Pallas kernels, body(): pl.pallas_call(finish_kernel, out_shape=jax.ShapeDtypeStruct(front.shape,...  4.33 us

profile of v6, /device:TPU:1, one launch (start us, length us, event | category | flops | bytes accessed | tf_op | source)
XLA Modules:
  0.0 65.9 jit_solution(6486038741176109276)
XLA Ops:
  0.0 61.6 %shard_map.91.got_hbm = bf16[4,4,256,256]{3,2,1,0:T(8,128)(2,1)} custom-call(s32[4,4]{1,0:T(4,128)} %bitcast.13, s32[1,64]{1,0:T(1,128)} %own_ref.1, s32[4,2,24]{2,1,0:T(2,128)} %slots_hbm.1, bf16[2,3,8,16,256]{4,3,2,1,0:T(8,128)(2,1)} %bitcast.8, bf16[2,2,64,256]{3,2,1,0:T(8,128)(2,1)} %bitcast.10, bf16[2,256,256]{2,1,0:T(8,128)(2,1)} %bitcast.9, ...), custom_call_target="tpu_custom_call" | custom-call | tf_op jit(solution)/shard_map/pallas_call | solution.py:504
  61.6 4.3 %shard_map.92 = f32[16,256,256]{2,1,0:T(8,128)} custom-call(f32[16,256,256]{2,1,0:T(8,128)} %front_hbm.1, bf16[4,4,256,256]{3,2,1,0:T(8,128)(2,1)} %shard_map.91.got_hbm), custom_call_target="tpu_custom_call" | custom-call | tf_op jit(solution)/shard_map/pallas_call | solution.py:559
